TPU v7x, 256 devices: a whole 4x4x8 slice. The times are simulated.
256 devices in a mesh: dp: 16 (over z, y_hi), tensor: 16 (over x, y_lo, core).
Axes of the slice: x: 4, y: 4 (y_hi: 2, y_lo: 2; y = y_hi * 2 + y_lo), z: 8, core: 2. Of those that a mesh axis runs over, the one named last changes fastest.
Arguments:
- inputs: bfloat16 [4096, 5120], P('dp'), may hold values from -6 to 6
- upstream: bfloat16 [4096, 5120], P('dp'), may hold values from -6 to 6
- w_in: bfloat16 [5120, 10240], P('dp', 'tensor'), may hold values from -0.125 to 0.125
- bias_in: bfloat16 [10240], P('tensor'), may hold values from -3 to 3
- w_out: bfloat16 [10240, 5120], P('tensor', 'dp'), may hold values from -0.0625 to 0.0625
Outputs:
- grad_inputs: bfloat16 [4096, 5120], P('dp', 'tensor')
- grad_w_in: float32 [5120, 10240], P('dp', 'tensor')
- grad_w_out: float32 [10240, 5120], P('tensor', 'dp')
All inputs are finite; a program needn't handle non-finite values.
Results may differ from a plain program's by a relative error of at most 0.022.
Values may be sent and summed in bfloat16 or wider, within the bound.
A program may use at most 128 MiB of HBM per device.

v0:
```python
import math

import jax
import jax.numpy as jnp
from jax import lax
from jax.sharding import PartitionSpec as P

root_half = 0.7071067811865476
inv_root_two_pi = 0.3989422804014327


def gelu_pair(pre_act):
    normal_cdf = 0.5 * (1.0 + lax.erf(pre_act * root_half))
    gelu_value = pre_act * normal_cdf
    gelu_slope = normal_cdf + pre_act * jnp.exp(-0.5 * pre_act * pre_act) * inv_root_two_pi
    return (gelu_value, gelu_slope)


def per_device(inputs, upstream, w_in, bias_in, w_out):
    tok_rows = inputs.shape[0]
    groups = lax.axis_size("dp")
    grad_scale = 1.0 / math.sqrt(tok_rows * groups)
    full_in = lax.all_gather(w_in, "dp", axis=0, tiled=True)
    pre_act = jnp.dot(inputs, full_in, preferred_element_type=jnp.float32)
    pre_act = pre_act + bias_in.astype(jnp.float32)
    gelu_value, gelu_slope = gelu_pair(pre_act)
    activated = gelu_value.astype(jnp.bfloat16)
    grad_act = lax.dot_general(
        upstream,
        lax.all_gather(w_out, "dp", axis=1, tiled=True),
        (((1,), (1,)), ((), ())),
        preferred_element_type=jnp.float32,
    )
    grad_pre = (grad_act * gelu_slope).astype(jnp.bfloat16)
    grad_w_in = lax.psum_scatter(
        (
            lax.dot_general(
                inputs, grad_pre, (((0,), (0,)), ((), ())), preferred_element_type=jnp.float32
            )
            * grad_scale
        ).astype(jnp.bfloat16),
        "dp",
        scatter_dimension=0,
        tiled=True,
    ).astype(jnp.float32)
    partial_x = lax.dot_general(
        grad_pre, full_in, (((1,), (1,)), ((), ())), preferred_element_type=jnp.float32
    )
    grad_inputs = lax.psum_scatter(
        partial_x.astype(jnp.bfloat16), "tensor", scatter_dimension=1, tiled=True
    )
    out_term = (
        lax.dot_general(
            activated, upstream, (((0,), (0,)), ((), ())), preferred_element_type=jnp.float32
        )
        * grad_scale
    )
    grad_w_out = lax.psum_scatter(
        out_term.astype(jnp.bfloat16), "dp", scatter_dimension=1, tiled=True
    ).astype(jnp.float32)
    return (grad_inputs, grad_w_in, grad_w_out)


def solution(mesh):
    placed = (P("dp", None), P("dp", None), P("dp", "tensor"), P("tensor"), P("tensor", "dp"))
    return jax.shard_map(
        per_device,
        mesh=mesh,
        in_specs=placed,
        out_specs=(P("dp", "tensor"), P("dp", "tensor"), P("tensor", "dp")),
        check_vma=False,
    )
```

profile of v0, /device:TPU:1, one launch (start us, length us, event | category | flops | bytes accessed | tf_op | source)
XLA Modules:
  0.0 767.9 jit_solution(8520685649337049828)
XLA Ops:
  7.2 0.0 copy-start
  7.2 0.0 all-gather.5.cloned.1.call-start
  7.2 0.7 all-gather.5.cloned.1.call-update
  7.9 0.0 all-gather.3.cloned.1.call-start
  8.0 0.7 all-gather.3.cloned.1.call-update
  8.7 0.0 reduce-scatter.12.cloned.1.call-start
  8.7 0.7 convert_element_type.27
  9.4 122.6 %all-gather.5.cloned.1.call-done = bf16[5120,640]{1,0:T(8,128)(2,1)} async-done(((bf16[320,640]{1,0:T(8,128)(2,1)}), bf16[5120,640]{1,0:T(8,128)(2,1)}) %all-gather.5.cloned.1.call-update) | async-done | bytes 6553616 | tf_op jit(solution)/shard_map/all_gather | solution.py:23
  132.0 5.9 convolution_add_fusion
  137.9 0.0 copy-start.2
  137.9 0.8 copy-done.2
  138.7 0.0 copy-done
  138.7 4.7 multiply_convert_fusion
  143.4 9.6 %copy.17 = bf16[640,5120]{0,1:T(8,128)(2,1)} copy(bf16[640,5120]{1,0:T(8,128)(2,1)} %multiply_convert_fusion) | data formatting | bytes 13107200
  153.0 0.0 reduce-scatter.12.cloned.1.call-update
  153.0 0.0 reduce-scatter.10.cloned.1.call-start
  153.1 96.5 %all-gather.3.cloned.1.call-done = bf16[640,5120]{0,1:T(8,128)(2,1)} async-done(((bf16[640,320]{0,1:T(8,128)(2,1)}), bf16[640,5120]{0,1:T(8,128)(2,1)}) %all-gather.3.cloned.1.call-update) | async-done | bytes 6553616 | tf_op jit(solution)/shard_map/all_gather | solution.py:30
  249.6 5.3 fusion.1
  254.9 0.0 copy-done.1
  254.9 4.7 fusion
  259.6 9.5 %copy.15 = bf16[5120,640]{1,0:T(8,128)(2,1)} copy(bf16[5120,640]{0,1:T(8,128)(2,1)} %fusion) | data formatting | bytes 13107200
  269.1 0.0 reduce-scatter.10.cloned.1.call-update
  269.1 0.0 reduce-scatter.8.cloned.1.call-start
  269.2 6.7 convolution_convert_fusion
  275.9 0.0 reduce-scatter.8.cloned.1.call-update
  275.9 192.9 %reduce-scatter.12.cloned.1.call-done = bf16[320,640]{1,0:T(8,128)(2,1)} async-done(((bf16[5120,640]{1,0:T(8,128)(2,1)}), bf16[320,640]{1,0:T(8,128)(2,1)}) %reduce-scatter.12.cloned.1.call-update) | async-done | bytes 409616
  468.8 1.3 copy.18
  470.1 1.1 copy.13
  471.2 221.2 %reduce-scatter.10.cloned.1.call-done = bf16[320,640]{1,0:T(8,128)(2,1)} async-done(((bf16[5120,640]{1,0:T(8,128)(2,1)}), bf16[320,640]{1,0:T(8,128)(2,1)}) %reduce-scatter.10.cloned.1.call-update) | async-done | bytes 409616
  692.4 1.3 copy.16
  693.7 1.1 copy.12
  694.8 66.6 %reduce-scatter.8.cloned.1.call-done = bf16[256,320]{0,1:T(8,128)(2,1)} async-done(((bf16[256,5120]{0,1:T(8,128)(2,1)}), bf16[256,320]{0,1:T(8,128)(2,1)}) %reduce-scatter.8.cloned.1.call-update) | async-done | bytes 163856 | tf_op jit(solution)/shard_map/reduce_scatter | solution.py:49
  (1 shorter events, 0.0 us)
Async XLA Ops:
  7.2 131.5 %copy-start = (bf16[256,5120]{1,0:T(8,128)(2,1)S(1)}, bf16[256,5120]{1,0:T(8,128)(2,1)}, u32[]{:S(2)}) copy-start(bf16[256,5120]{1,0:T(8,128)(2,1)} %param.6) | copy-start | bytes 7864324
  7.2 124.8 %all-gather.5.cloned.1.call-start = ((), (), s32[]{:S(2)}) async-start(), calls=%async_computation.4 | async-start | bytes 6963200 | tf_op jit(solution)/shard_map/all_gather | solution.py:23
  7.9 241.6 %all-gather.3.cloned.1.call-start = ((), (), s32[]{:S(2)}) async-start(), calls=%async_computation.3 | async-start | bytes 6963200 | tf_op jit(solution)/shard_map/all_gather | solution.py:30
  8.7 460.1 %reduce-scatter.12.cloned.1.call-start = ((), (), s32[]{:S(2)}) async-start(), calls=%async_computation.7 | async-start | bytes 6963200
  137.9 0.8 copy-start.2
  153.0 539.4 %reduce-scatter.10.cloned.1.call-start = ((), (), s32[]{:S(2)}) async-start(), calls=%async_computation.6 | async-start | bytes 6963200
  249.6 5.3 copy-start.1
  269.1 492.2 %reduce-scatter.8.cloned.1.call-start = ((), (), s32[]{:S(2)}) async-start(), calls=%async_computation.5 | async-start | bytes 2785280 | tf_op jit(solution)/shard_map/reduce_scatter | solution.py:49
Sparse Core Ops, SparseCore 0:
  10.6 121.3 all-gather.4
  134.6 114.9 all-gather.2
  253.7 215.0 reduce-scatter.11
  472.8 219.5 reduce-scatter.9
  695.4 65.9 reduce-scatter.7
where the time goes:
time: 771 us; the launch traced here: 768 us
  waiting for transfers between devices  701 us (91%)
  matrix products  27.3 us (4%)
  local copies, waits for them, and re-layouts  24.7 us (3%)
  between operations  13.8 us (2%)
    unnamed x7, waiting for transfers between devices  416 us
    all_gather x1, waiting for transfers between devices, per_device(): full_in = lax.all_gather(w_in, 'dp', axis=0, tiled=True)  123 us
    all_gather x1, waiting for transfers between devices, per_device(): lax.all_gather(w_out, 'dp', axis=1, tiled=True)  96.5 us
    reduce_scatter x1, waiting for transfers between devices, per_device(): lax.psum_scatter(partial_x.astype(jnp.bfloat16), 'tensor', scatter_dimens...  66.6 us
    unnamed x12, local copies, waits for them, and re-layouts  24.7 us
  transfers between devices with their start and end apart: 5, of which 5 were waited for; matrix products, arithmetic and copies ran while one was open for 7% of the time, Pallas kernels for 0%

commit v1 on v0

v1 whole, which is shorter than its diff:
```python
import math

import jax
import jax.numpy as jnp
from jax import lax
from jax.experimental import pallas as pl
from jax.experimental.pallas import tpu as pltpu
from jax.sharding import PartitionSpec as P

MESH = pl.DeviceIdType.MESH
ROOT_HALF = 0.7071067811865476
INV_ROOT_TWO_PI = 0.3989422804014327
BF16 = jnp.bfloat16
F32 = jnp.float32

NZ = 8
NT = 8
ROWS = 256
SH = 320
HF = SH // 2
FC = 640
A = pl.ds(0, HF)
B = pl.ds(HF, HF)
FULL = pl.ds(0, SH)

TN = (((0,), (0,)), ((), ()))
NN = (((1,), (0,)), ((), ()))
NT_DIMS = (((1,), (1,)), ((), ()))


def dot(lhs, rhs, dims):
    return lax.dot_general(lhs, rhs, dims, preferred_element_type=F32)


def kernel(
    scale, x_hbm, dy_hbm, win_hbm, wout_hbm, bias_ref,
    dx_out, dwin_out, dwout_out,
    xv, dyv, wov, wt, xt, dyt, wi, wo,
    pre, pre_in, act, ga, ga_in, gp, slope,
    term_o, term_i, rin_o, rin_i, lin_o, lin_i, own_o, own_i,
    dxs, dxr, bias_in,
    ld_sem, sw_s, sw_r, ag_s, ag_r, ex_s, ex_r, core_s, core_r,
    rs_s, rs_r, own_s, own_r, dx_s, dx_r,
):
    dp = lax.axis_index("dp")
    tn = lax.axis_index("tensor")
    z, a = lax.div(dp, 2), lax.rem(dp, 2)
    t2, b = lax.div(tn, 2), lax.rem(tn, 2)
    xpar = lax.rem(lax.div(t2, 2), 2)
    ypar = lax.rem(t2, 2)
    same = a == b
    zr, zl = lax.rem(z + 1, NZ), lax.rem(z + NZ - 1, NZ)

    def dev(z_, t_, a_, b_):
        return {"dp": 2 * z_ + a_, "tensor": 2 * t_ + b_}

    right, left = dev(zr, t2, a, b), dev(zl, t2, a, b)
    swap, swap_r, swap_l = dev(z, t2, b, a), dev(zr, t2, b, a), dev(zl, t2, b, a)
    other_core = dev(z, t2, a, 1 - b)
    y_side = dev(z, t2 + 1 - 2 * ypar, 1 - a, b)
    x_side = dev(z, t2 + 2 - 4 * xpar, a, b)

    def rc(src, dst, ss, rs, to):
        return pltpu.make_async_remote_copy(
            src_ref=src, dst_ref=dst, send_sem=ss, recv_sem=rs, device_id=to, device_id_type=MESH
        )

    ld_x = pltpu.make_async_copy(x_hbm, xv, ld_sem.at[0])
    ld_dy = pltpu.make_async_copy(dy_hbm, dyv, ld_sem.at[1])
    ld_wo = pltpu.make_async_copy(wout_hbm, wov, ld_sem.at[2])
    ld_wi = pltpu.make_async_copy(win_hbm, wi.at[0], ld_sem.at[3])
    pl.when(same)(ld_wi.start)
    ld_wo.start()
    ld_x.start()
    ld_dy.start()

    barrier = pltpu.get_barrier_semaphore()

    def greet(to):
        pl.semaphore_signal(barrier, inc=1, device_id=to, device_id_type=MESH)

    plane = [(r, q) for r in range(NT) for q in range(2) if (r, q) != (0, 0)]

    def flip(q):
        return a + q - 2 * a * q

    def plane_dev(r, q):
        return dev(z, lax.rem(t2 + r, NT), flip(q), b)

    greet(right)
    greet(left)
    greet(other_core)
    for r, q in plane:
        greet(plane_dev(r, q))

    @pl.when(jnp.logical_not(same))
    def _():
        greet(swap)
        greet(swap_r)
        greet(swap_l)

    @pl.when(same)
    def _():
        pl.semaphore_wait(barrier, 18)

    @pl.when(jnp.logical_not(same))
    def _():
        pl.semaphore_wait(barrier, 21)

    weights = (wi, wo)

    def ag(w, g, s, rows, part):
        buf = weights[w]
        if g == 0:
            src, dst, to = s - 1, s, right
        else:
            src, dst, to = (NZ + 1 - s) % NZ, NZ - s, left
        i = ((w * 2 + g) * 4 + s - 1) * 2 + part
        return rc(buf.at[src, rows], buf.at[dst, rows], ag_s.at[i], ag_r.at[i], to)

    swap_wi = rc(win_hbm, wi.at[0], sw_s.at[0], sw_r.at[0], swap)
    swap_wo = rc(wt, wo.at[0], sw_s.at[1], sw_r.at[1], swap)

    @pl.when(same)
    def _():
        ld_wi.wait()
        ag(0, 0, 1, FULL, 0).start()
        ag(0, 1, 1, FULL, 0).start()

    @pl.when(jnp.logical_not(same))
    def _():
        swap_wi.start()

    bias_in[0] = jnp.broadcast_to(bias_ref[...].astype(F32), (8, FC))
    bias_cp = rc(bias_in.at[0], bias_in.at[1], core_s.at[2], core_r.at[2], other_core)
    bias_cp.start()

    ld_wo.wait()
    w_t = wov[...].T

    @pl.when(same)
    def _():
        wo[0] = w_t
        ag(1, 0, 1, FULL, 0).start()
        ag(1, 1, 1, FULL, 0).start()

    @pl.when(jnp.logical_not(same))
    def _():
        wt[...] = w_t
        swap_wo.start()

    pairs = ((0, 1), (7, 2), (6, 3), (5, 4))

    def mine(i):
        p, q = pairs[i]
        return p + (q - p) * xpar

    def theirs(i):
        p, q = pairs[i]
        return q + (p - q) * xpar

    def turn(src, dst, d):
        k = lax.rem(z + NZ - d, NZ)
        v = src[:, pl.ds(pl.multiple_of(k * 2 * SH, 128), 2 * SH)].T
        dst[d, a] = jnp.where(b == 0, v[:SH], v[SH:])

    rows_t = (xt, dyt)

    def ex_y(w, i):
        buf, d, m = rows_t[w], mine(i), w * 8 + i
        return rc(buf.at[d, a], buf.at[d, a], ex_s.at[m], ex_r.at[m], y_side)

    def ex_y_in(w, i):
        buf, d, m = rows_t[w], mine(i), w * 8 + i
        return rc(buf.at[d, 1 - a], buf.at[d, 1 - a], ex_s.at[m], ex_r.at[m], y_side)

    def ex_x(w, i):
        buf, d, m = rows_t[w], mine(i), w * 8 + 4 + i
        return rc(buf.at[d, 1 - a], buf.at[d, 1 - a], ex_s.at[m], ex_r.at[m], x_side)

    def ex_x_in(w, i):
        buf, d, m = rows_t[w], theirs(i), w * 8 + 4 + i
        return rc(buf.at[d, 1 - a], buf.at[d, 1 - a], ex_s.at[m], ex_r.at[m], x_side)

    ld_x.wait()
    for i in range(4):
        turn(xv, xt, pairs[i][0])
        turn(xv, xt, pairs[i][1])
        ex_y(0, i).start()

    @pl.when(jnp.logical_not(same))
    def _():
        swap_wi.wait_recv()
        ag(0, 0, 1, FULL, 0).start()
        ag(0, 1, 1, FULL, 0).start()
        swap_wo.wait_recv()
        ag(1, 0, 1, FULL, 0).start()
        ag(1, 1, 1, FULL, 0).start()

    ld_dy.wait()
    for i in range(4):
        turn(dyv, dyt, pairs[i][0])
        turn(dyv, dyt, pairs[i][1])
        ex_y(1, i).start()

    def pass_on(w, i):
        ex_y_in(w, i).wait_recv()
        ex_x(w, i).start()

    def step(w, s, nxt):
        for g in range(2):
            ag(w, g, s, FULL, 0).wait_recv()
            for rows, part in nxt[g]:
                ag(w, g, s + 1, rows, part).start()

    whole = [[(FULL, 0)], [(FULL, 0)]]

    def accumulate(acc, src, w, slots, first=False):
        n = len(slots)

        def body(i, carry):
            j, h = lax.div(i, 2), lax.rem(i, 2)
            d = slots[0] if n == 1 else slots[0] + j * (slots[1] - slots[0])
            acc[h] += dot(src[d, h], w[d], TN)
            return carry

        if first:
            acc[...] = jnp.zeros_like(acc)
        lax.fori_loop(0, 2 * n, body, 0)

    step(0, 1, whole)
    pass_on(0, 0)
    pass_on(0, 1)
    step(1, 1, whole)
    pass_on(0, 2)
    pass_on(0, 3)
    step(0, 2, whole)
    for i in range(2):
        ex_x_in(0, i).wait_recv()
    accumulate(pre, xt, wi, (0,), True)
    accumulate(pre, xt, wi, (1, 7))
    pass_on(1, 0)
    pass_on(1, 1)
    step(1, 2, [[(A, 0), (B, 1)], [(B, 0), (A, 1)]])
    for i in range(2, 4):
        ex_x_in(0, i).wait_recv()
    accumulate(pre, xt, wi, (2, 6))
    pass_on(1, 2)
    pass_on(1, 3)
    step(0, 3, [[(A, 0)], [(B, 0)]])
    accumulate(pre, xt, wi, (3, 5))
    for i in range(4):
        ex_x_in(1, i).wait_recv()
    accumulate(ga, dyt, wo, (0,), True)
    accumulate(ga, dyt, wo, (1, 7))
    accumulate(ga, dyt, wo, (2, 6))
    ag(1, 0, 3, A, 0).wait_recv()
    ag(1, 0, 4, A, 0).start()
    ag(1, 1, 3, B, 0).wait_recv()
    ag(1, 1, 4, B, 0).start()
    ag(0, 0, 4, A, 0).wait_recv()
    ag(0, 1, 4, B, 0).wait_recv()
    accumulate(pre, xt, wi, (4,))
    pre_cp = rc(pre, pre_in, core_s.at[0], core_r.at[0], other_core)
    pre_cp.start()
    bias_cp.wait_recv()
    bias = jnp.where(same, bias_in[0], bias_in[1])[0:1]
    pre_cp.wait_recv()

    def gelu(i, carry):
        h, rows = lax.div(i, 8), pl.ds(pl.multiple_of(lax.rem(i, 8) * 32, 32), 32)
        v = pre[h, rows] + pre_in[h, rows] + bias
        cdf = 0.5 * (1.0 + lax.erf(v * ROOT_HALF))
        act[h, rows] = (v * cdf).astype(BF16)
        slope[h, rows] = cdf + v * jnp.exp(-0.5 * v * v) * INV_ROOT_TWO_PI
        return carry

    lax.fori_loop(0, 16, gelu, 0)

    terms, rins, lins, owns = (term_o, term_i), (rin_o, rin_i), (lin_o, lin_i), (own_o, own_i)

    def make_terms(w, lo, hi):
        src, val, out = (dyt, xt)[w], (act, gp)[w], terms[w]

        def body(i, carry):
            d = lax.rem(4 + lax.div(i + 1, 2) * (2 * lax.rem(i, 2) - 1) + NZ, NZ)
            total = dot(src[d, 0], val[0], NN) + dot(src[d, 1], val[1], NN)
            out[d] = (total * scale).astype(BF16)
            return carry

        lax.fori_loop(lo, hi, body, 0)

    def rs(w, g, e, rows, part):
        buf = terms[w]
        d = NZ - e if g == 0 else e
        to = (right, left)[g] if e > 1 else (swap_r, swap_l)[g]
        dst = (rins, lins)[g][w]
        i = ((w * 2 + g) * 4 + e - 1) * 2 + part
        return rc(buf.at[d, rows], dst.at[e - 1, rows], rs_s.at[i], rs_r.at[i], to)

    def add_in(w, g, e, rows):
        d = NZ - e if g == 0 else e
        came = (rins, lins)[g][w]
        buf = terms[w]
        buf[d, rows] = (buf[d, rows].astype(F32) + came[e, rows].astype(F32)).astype(BF16)

    def hop(w, g, e, rows, part, rows_in=None, part_in=None):
        rs(w, g, e + 1, rows, part if part_in is None else part_in).wait_recv()
        add_in(w, g, e, rows)
        rs(w, g, e, rows, part).start()

    firsts = (A, B)
    seconds = (B, A)

    def own_copy(w):
        i = w
        return rc(terms[w].at[0], owns[w], own_s.at[i], own_r.at[i], swap)

    def own_local(w):
        return pltpu.make_async_copy(terms[w].at[0], owns[w], own_s.at[2 + w])

    def send_own(w):
        @pl.when(same)
        def _():
            own_local(w).start()

        @pl.when(jnp.logical_not(same))
        def _():
            own_copy(w).start()

    def wait_own(w):
        @pl.when(same)
        def _():
            own_local(w).wait()

        @pl.when(jnp.logical_not(same))
        def _():
            own_copy(w).wait()

    make_terms(0, 0, 3)
    for g in range(2):
        rs(0, g, 4, firsts[g], 0).start()
    for g in range(2):
        rs(0, g, 3, seconds[g], 1).start()
    ag(1, 0, 3, B, 1).wait_recv()
    ag(1, 1, 3, A, 1).wait_recv()
    accumulate(ga, dyt, wo, (3, 5))
    ag(1, 0, 4, A, 0).wait_recv()
    ag(1, 1, 4, B, 0).wait_recv()
    accumulate(ga, dyt, wo, (4,))
    ga_cp = rc(ga, ga_in, core_s.at[1], core_r.at[1], other_core)
    ga_cp.start()
    for g in range(2):
        hop(0, g, 3, firsts[g], 0)
    make_terms(0, 3, 8)
    send_own(0)
    ga_cp.wait_recv()

    def grad(i, carry):
        h, rows = lax.div(i, 8), pl.ds(pl.multiple_of(lax.rem(i, 8) * 32, 32), 32)
        gp[h, rows] = ((ga[h, rows] + ga_in[h, rows]) * slope[h, rows]).astype(BF16)
        return carry

    lax.fori_loop(0, 16, grad, 0)
    make_terms(1, 0, 3)
    for g in range(2):
        rs(1, g, 4, firsts[g], 0).start()
    for g in range(2):
        rs(1, g, 3, seconds[g], 1).start()
    make_terms(1, 3, 8)
    send_own(1)

    def dx_body(i, carry):
        d, h = lax.div(i, 2), lax.rem(i, 2)
        dxs[d, h] = dot(wi[d], gp[h], NT_DIMS).astype(BF16)
        return carry

    lax.fori_loop(0, 16, dx_body, 0)

    def dx_cp(r, q):
        d = lax.rem(z + 2 * NZ - lax.rem(t2 + r, NT), NZ)
        m = 2 * r + q
        return rc(dxs.at[d, flip(q)], dxr.at[m], dx_s.at[m], dx_r.at[m], plane_dev(r, q))

    for r, q in plane:
        dx_cp(r, q).start()

    def both_halves(w, e):
        for g in range(2):
            rs(w, g, e + 1, seconds[g], 1).wait_recv()
            rs(w, g, e + 1, firsts[g], 0).wait_recv()
            add_in(w, g, e, FULL)
            rs(w, g, e, FULL, 0).start()

    both_halves(0, 2)
    for g in range(2):
        hop(1, g, 3, firsts[g], 0)
    for g in range(2):
        rs(0, g, 2, FULL, 0).wait_recv()
        add_in(0, g, 1, FULL)
        rs(0, g, 1, FULL, 0).start()
    for part, pick in ((1, seconds), (0, firsts)):
        for g in range(2):
            hop(1, g, 2, pick[g], part)

    for r, q in plane:
        dx_cp(r, q).wait_recv()
    mine_d = lax.rem(z + NZ - t2, NZ)
    total = dxs[mine_d, a].astype(F32)
    for r, q in plane:
        total = total + dxr[2 * r + q].astype(F32)
    dx_out[...] = total.T.astype(BF16)

    for part, pick in ((1, seconds), (0, firsts)):
        for g in range(2):
            hop(1, g, 1, pick[g], part)

    wait_own(0)
    for g in range(2):
        rs(0, g, 1, FULL, 0).wait_recv()
    dw = own_o[...].astype(F32) + rin_o[0].astype(F32) + lin_o[0].astype(F32)
    dwout_out[...] = dw.T

    wait_own(1)
    for part, pick in ((1, seconds), (0, firsts)):
        for g in range(2):
            rs(1, g, 1, pick[g], part).wait_recv()
    dwin_out[...] = own_i[...].astype(F32) + rin_i[0].astype(F32) + lin_i[0].astype(F32)

    @pl.when(jnp.logical_not(same))
    def _():
        swap_wi.wait_send()
        swap_wo.wait_send()

    for w in range(2):
        for g in range(2):
            ag(w, g, 1, FULL, 0).wait_send()
            ag(w, g, 2, FULL, 0).wait_send()
            ag(w, g, 4, firsts[g], 0).wait_send()
        for i in range(4):
            ex_y(w, i).wait_send()
            ex_x(w, i).wait_send()
    for g in range(2):
        ag(0, g, 3, FULL, 0).wait_send()
        ag(1, g, 3, firsts[g], 0).wait_send()
        ag(1, g, 3, seconds[g], 1).wait_send()
    bias_cp.wait_send()
    pre_cp.wait_send()
    ga_cp.wait_send()
    for w in range(2):
        for g in range(2):
            rs(w, g, 4, firsts[g], 0).wait_send()
            rs(w, g, 3, seconds[g], 1).wait_send()
            rs(w, g, 3, firsts[g], 0).wait_send()
    for g in range(2):
        rs(0, g, 2, FULL, 0).wait_send()
        rs(0, g, 1, FULL, 0).wait_send()
        for e in (2, 1):
            rs(1, g, e, seconds[g], 1).wait_send()
            rs(1, g, e, firsts[g], 0).wait_send()
    for r, q in plane:
        dx_cp(r, q).wait_send()


def per_device(inputs, upstream, w_in, bias_in, w_out):
    rows, width = inputs.shape
    scale = 1.0 / math.sqrt(rows * lax.axis_size("dp"))
    any_space = pl.BlockSpec(memory_space=pl.ANY)
    vmem = pl.BlockSpec(memory_space=pltpu.VMEM)
    shard = (SH, FC)
    ring = (NZ,) + shard
    acc = (2, ROWS, FC)
    turned = (NZ, 2, SH, ROWS)
    return pl.pallas_call(
        lambda *refs: kernel(scale, *refs),
        out_shape=(
            jax.ShapeDtypeStruct((ROWS, SH), BF16),
            jax.ShapeDtypeStruct((SH, FC), F32),
            jax.ShapeDtypeStruct((FC, SH), F32),
        ),
        in_specs=[any_space, any_space, any_space, any_space, vmem],
        out_specs=(vmem, vmem, vmem),
        scratch_shapes=[
            pltpu.VMEM((rows, width), BF16),
            pltpu.VMEM((rows, width), BF16),
            pltpu.VMEM((FC, SH), BF16),
            pltpu.VMEM(shard, BF16),
            pltpu.VMEM(turned, BF16),
            pltpu.VMEM(turned, BF16),
            pltpu.VMEM(ring, BF16),
            pltpu.VMEM(ring, BF16),
            pltpu.VMEM(acc, F32),
            pltpu.VMEM(acc, F32),
            pltpu.VMEM(acc, BF16),
            pltpu.VMEM(acc, F32),
            pltpu.VMEM(acc, F32),
            pltpu.VMEM(acc, BF16),
            pltpu.VMEM(acc, F32),
            pltpu.VMEM(ring, BF16),
            pltpu.VMEM(ring, BF16),
            pltpu.VMEM((4,) + shard, BF16),
            pltpu.VMEM((4,) + shard, BF16),
            pltpu.VMEM((4,) + shard, BF16),
            pltpu.VMEM((4,) + shard, BF16),
            pltpu.VMEM(shard, BF16),
            pltpu.VMEM(shard, BF16),
            pltpu.VMEM(turned, BF16),
            pltpu.VMEM((16, SH, ROWS), BF16),
            pltpu.VMEM((2, 8, FC), F32),
            pltpu.SemaphoreType.DMA((4,)),
            pltpu.SemaphoreType.DMA((2,)),
            pltpu.SemaphoreType.DMA((2,)),
            pltpu.SemaphoreType.DMA((32,)),
            pltpu.SemaphoreType.DMA((32,)),
            pltpu.SemaphoreType.DMA((16,)),
            pltpu.SemaphoreType.DMA((16,)),
            pltpu.SemaphoreType.DMA((3,)),
            pltpu.SemaphoreType.DMA((3,)),
            pltpu.SemaphoreType.DMA((32,)),
            pltpu.SemaphoreType.DMA((32,)),
            pltpu.SemaphoreType.DMA((4,)),
            pltpu.SemaphoreType.DMA((4,)),
            pltpu.SemaphoreType.DMA((16,)),
            pltpu.SemaphoreType.DMA((16,)),
        ],
        compiler_params=pltpu.CompilerParams(
            collective_id=0, has_side_effects=True, vmem_limit_bytes=60 * 1024 * 1024
        ),
    )(inputs, upstream, w_in, w_out, bias_in.reshape(1, -1))


def solution(mesh):
    placed = (P("dp", None), P("dp", None), P("dp", "tensor"), P("tensor"), P("tensor", "dp"))
    return jax.shard_map(
        per_device,
        mesh=mesh,
        in_specs=placed,
        out_specs=(P("dp", "tensor"), P("dp", "tensor"), P("tensor", "dp")),
        check_vma=False,
    )
```

time: 771 us -> 163 us (0.21)
  the two profiles are of different devices: /device:TPU:1 before, /device:TPU:45 now
where the time goes in v1:
time: 163 us
  Pallas kernels  154 us (94%)
  local copies, waits for them, and re-layouts  8.34 us (5%)
    pallas_call x1, Pallas kernels, per_device(): pl.pallas_call(lambda *refs: kernel(scale, *refs), out_shape=(jax.ShapeDt...  154 us
    pallas_call x2, local copies, waits for them, and re-layouts, per_device(): pl.pallas_call(lambda *refs: kernel(scale, *refs), out_shape=(jax.ShapeDt...  4.2 us

profile of v1, /device:TPU:45, one launch (start us, length us, event | category | flops | bytes accessed | tf_op | source)
XLA Modules:
  0.0 163.1 jit_solution(3410874751387084796)
XLA Ops:
  0.6 1.3 reshape.9.refs_4_
  1.9 2.0 %copy.8.refs_3_ = bf16[640,320]{1,0:T(8,128)(2,1)} copy(bf16[640,320]{0,1:T(8,128)(2,1)} %param.9) | data formatting | bytes 819200 | tf_op args[4]
  3.9 154.1 %shard_map.76 = (bf16[256,320]{1,0:T(8,128)(2,1)}, f32[320,640]{1,0:T(8,128)}, f32[640,320]{1,0:T(8,128)}) custom-call(bf16[256,5120]{1,0:T(8,128)(2,1)} %refs_0_.1, bf16[256,5120]{1,0:T(8,128)(2,1)} %refs_1_.1, bf16[320,640]{1,0:T(8,128)(2,1)} %refs_2_.1, bf16[640,320]{1,0:T(8,128)(2,1)} %copy.8.refs_3_, bf16[1,640]{1,0:T(2,128)(2,1)} %reshape.9.refs_4_), custom_call_target="tpu_custom_call" | custom-call | tf_op jit(solution)/shard_map/pallas_call | solution.py:474
  158.0 0.0 copy-start
  158.0 1.8 %copy.9 = bf16[256,320]{0,1:T(8,128)(2,1)} copy(bf16[256,320]{1,0:T(8,128)(2,1)} %get-tuple-element.3) | data formatting | bytes 327680 | tf_op jit(solution)/shard_map/pallas_call | solution.py:474
  159.8 2.4 %copy.10 = f32[640,320]{0,1:T(8,128)} copy(f32[640,320]{1,0:T(8,128)} %get-tuple-element.5) | data formatting | bytes 1638400 | tf_op jit(solution)/shard_map/pallas_call | solution.py:474
  162.2 0.0 copy-done
  162.2 0.9 copy.12
Async XLA Ops:
  158.0 4.2 %copy-start = (f32[320,640]{1,0:T(8,128)S(1)}, f32[320,640]{1,0:T(8,128)}, u32[]{:S(2)}) copy-start(f32[320,640]{1,0:T(8,128)} %get-tuple-element.10) | copy-start | bytes 2457604

commit v2 on v1

--- a/solution.py
+++ b/solution.py
@@ -34,11 +34,11 @@
 
 def kernel(
     scale, x_hbm, dy_hbm, win_hbm, wout_hbm, bias_ref,
-    dx_out, dwin_out, dwout_out,
-    xv, dyv, wov, wt, xt, dyt, wi, wo,
+    dx_out, parts_i, parts_o,
+    dx_v, xv, dyv, xt, dyt, wi, wo,
     pre, pre_in, act, ga, ga_in, gp, slope,
-    term_o, term_i, rin_o, rin_i, lin_o, lin_i, own_o, own_i,
-    dxs, dxr, bias_in,
+    term_o, term_i, rin_o, rin_i, lin_o, lin_i,
+    dxs, x_in, ys, y_in, bias_in,
     ld_sem, sw_s, sw_r, ag_s, ag_r, ex_s, ex_r, core_s, core_r,
     rs_s, rs_r, own_s, own_r, dx_s, dx_r,
 ):
@@ -67,31 +67,46 @@
 
     ld_x = pltpu.make_async_copy(x_hbm, xv, ld_sem.at[0])
     ld_dy = pltpu.make_async_copy(dy_hbm, dyv, ld_sem.at[1])
-    ld_wo = pltpu.make_async_copy(wout_hbm, wov, ld_sem.at[2])
-    ld_wi = pltpu.make_async_copy(win_hbm, wi.at[0], ld_sem.at[3])
-    pl.when(same)(ld_wi.start)
-    ld_wo.start()
+    ld_wi = pltpu.make_async_copy(win_hbm, wi.at[0], ld_sem.at[2])
+    ld_wo = pltpu.make_async_copy(wout_hbm, wo.at[0], ld_sem.at[3])
+
+    @pl.when(same)
+    def _():
+        ld_wi.start()
+        ld_wo.start()
+
     ld_x.start()
     ld_dy.start()
 
+    put_dx = pltpu.make_async_copy(dx_v, dx_out, ld_sem.at[4])
+
     barrier = pltpu.get_barrier_semaphore()
 
     def greet(to):
         pl.semaphore_signal(barrier, inc=1, device_id=to, device_id_type=MESH)
 
-    plane = [(r, q) for r in range(NT) for q in range(2) if (r, q) != (0, 0)]
-
-    def flip(q):
-        return a + q - 2 * a * q
-
-    def plane_dev(r, q):
-        return dev(z, lax.rem(t2 + r, NT), flip(q), b)
+    x_, y_ = lax.div(t2, 2), 2 * a + ypar
+
+    def x_peer(r):
+        return lax.rem(x_ + r, 4)
+
+    def y_peer(r):
+        yy = lax.rem(y_ + r, 4)
+        return lax.rem(yy, 2), lax.div(yy, 2)
+
+    def x_dev(r):
+        return dev(z, 2 * x_peer(r) + ypar, a, b)
+
+    def y_dev(r):
+        yl, ah = y_peer(r)
+        return dev(z, 2 * x_ + yl, ah, b)
 
     greet(right)
     greet(left)
     greet(other_core)
-    for r, q in plane:
-        greet(plane_dev(r, q))
+    for r in (1, 2, 3):
+        greet(x_dev(r))
+        greet(y_dev(r))
 
     @pl.when(jnp.logical_not(same))
     def _():
@@ -101,11 +116,11 @@
 
     @pl.when(same)
     def _():
-        pl.semaphore_wait(barrier, 18)
+        pl.semaphore_wait(barrier, 9)
 
     @pl.when(jnp.logical_not(same))
     def _():
-        pl.semaphore_wait(barrier, 21)
+        pl.semaphore_wait(barrier, 12)
 
     weights = (wi, wo)
 
@@ -119,35 +134,26 @@
         return rc(buf.at[src, rows], buf.at[dst, rows], ag_s.at[i], ag_r.at[i], to)
 
     swap_wi = rc(win_hbm, wi.at[0], sw_s.at[0], sw_r.at[0], swap)
-    swap_wo = rc(wt, wo.at[0], sw_s.at[1], sw_r.at[1], swap)
+    swap_wo = rc(wout_hbm, wo.at[0], sw_s.at[1], sw_r.at[1], swap)
 
     @pl.when(same)
     def _():
         ld_wi.wait()
         ag(0, 0, 1, FULL, 0).start()
         ag(0, 1, 1, FULL, 0).start()
+        ld_wo.wait()
+        ag(1, 0, 1, FULL, 0).start()
+        ag(1, 1, 1, FULL, 0).start()
 
     @pl.when(jnp.logical_not(same))
     def _():
         swap_wi.start()
-
-    bias_in[0] = jnp.broadcast_to(bias_ref[...].astype(F32), (8, FC))
+        swap_wo.start()
+
+    bias_in[0] = jnp.broadcast_to(bias_ref[...].astype(F32)[None, :], (8, FC))
     bias_cp = rc(bias_in.at[0], bias_in.at[1], core_s.at[2], core_r.at[2], other_core)
     bias_cp.start()
 
-    ld_wo.wait()
-    w_t = wov[...].T
-
-    @pl.when(same)
-    def _():
-        wo[0] = w_t
-        ag(1, 0, 1, FULL, 0).start()
-        ag(1, 1, 1, FULL, 0).start()
-
-    @pl.when(jnp.logical_not(same))
-    def _():
-        wt[...] = w_t
-        swap_wo.start()
 
     pairs = ((0, 1), (7, 2), (6, 3), (5, 4))
 
@@ -277,7 +283,7 @@
 
     lax.fori_loop(0, 16, gelu, 0)
 
-    terms, rins, lins, owns = (term_o, term_i), (rin_o, rin_i), (lin_o, lin_i), (own_o, own_i)
+    terms, rins, lins, ends = (term_o, term_i), (rin_o, rin_i), (lin_o, lin_i), (parts_o, parts_i)
 
     def make_terms(w, lo, hi):
         src, val, out = (dyt, xt)[w], (act, gp)[w], terms[w]
@@ -294,15 +300,15 @@
         buf = terms[w]
         d = NZ - e if g == 0 else e
         to = (right, left)[g] if e > 1 else (swap_r, swap_l)[g]
-        dst = (rins, lins)[g][w]
+        dst = (rins, lins)[g][w].at[e - 2] if e > 1 else ends[w].at[1 + g]
         i = ((w * 2 + g) * 4 + e - 1) * 2 + part
-        return rc(buf.at[d, rows], dst.at[e - 1, rows], rs_s.at[i], rs_r.at[i], to)
+        return rc(buf.at[d, rows], dst.at[rows], rs_s.at[i], rs_r.at[i], to)
 
     def add_in(w, g, e, rows):
         d = NZ - e if g == 0 else e
         came = (rins, lins)[g][w]
         buf = terms[w]
-        buf[d, rows] = (buf[d, rows].astype(F32) + came[e, rows].astype(F32)).astype(BF16)
+        buf[d, rows] = (buf[d, rows].astype(F32) + came[e - 1, rows].astype(F32)).astype(BF16)
 
     def hop(w, g, e, rows, part, rows_in=None, part_in=None):
         rs(w, g, e + 1, rows, part if part_in is None else part_in).wait_recv()
@@ -314,10 +320,10 @@
 
     def own_copy(w):
         i = w
-        return rc(terms[w].at[0], owns[w], own_s.at[i], own_r.at[i], swap)
+        return rc(terms[w].at[0], ends[w].at[0], own_s.at[i], own_r.at[i], swap)
 
     def own_local(w):
-        return pltpu.make_async_copy(terms[w].at[0], owns[w], own_s.at[2 + w])
+        return pltpu.make_async_copy(terms[w].at[0], ends[w].at[0], own_s.at[2 + w])
 
     def send_own(w):
         @pl.when(same)
@@ -371,19 +377,22 @@
     send_own(1)
 
     def dx_body(i, carry):
-        d, h = lax.div(i, 2), lax.rem(i, 2)
-        dxs[d, h] = dot(wi[d], gp[h], NT_DIMS).astype(BF16)
+        k, h = lax.div(i, 2), lax.rem(i, 2)
+        d = lax.rem(z + NZ - k, NZ)
+        dxs[lax.div(k, 2), 2 * lax.rem(k, 2) + h] = dot(wi[d], gp[h], NT_DIMS).astype(BF16)
         return carry
 
     lax.fori_loop(0, 16, dx_body, 0)
 
-    def dx_cp(r, q):
-        d = lax.rem(z + 2 * NZ - lax.rem(t2 + r, NT), NZ)
-        m = 2 * r + q
-        return rc(dxs.at[d, flip(q)], dxr.at[m], dx_s.at[m], dx_r.at[m], plane_dev(r, q))
-
-    for r, q in plane:
-        dx_cp(r, q).start()
+    def x_sum(r):
+        return rc(dxs.at[x_peer(r)], x_in.at[r - 1], dx_s.at[r - 1], dx_r.at[r - 1], x_dev(r))
+
+    def y_sum(r):
+        yl, ah = y_peer(r)
+        return rc(ys.at[2 * yl + ah], y_in.at[r - 1], dx_s.at[r + 2], dx_r.at[r + 2], y_dev(r))
+
+    for r in (1, 2, 3):
+        x_sum(r).start()
 
     def both_halves(w, e):
         for g in range(2):
@@ -403,29 +412,40 @@
         for g in range(2):
             hop(1, g, 2, pick[g], part)
 
-    for r, q in plane:
-        dx_cp(r, q).wait_recv()
-    mine_d = lax.rem(z + NZ - t2, NZ)
-    total = dxs[mine_d, a].astype(F32)
-    for r, q in plane:
-        total = total + dxr[2 * r + q].astype(F32)
-    dx_out[...] = total.T.astype(BF16)
+    for r in (1, 2, 3):
+        x_sum(r).wait_recv()
+
+    def x_body(i, carry):
+        total = dxs[x_, i].astype(F32)
+        for r in range(3):
+            total = total + x_in[r, i].astype(F32)
+        ys[i] = total.astype(BF16)
+        return carry
+
+    lax.fori_loop(0, 4, x_body, 0)
+    for r in (1, 2, 3):
+        y_sum(r).start()
 
     for part, pick in ((1, seconds), (0, firsts)):
         for g in range(2):
             hop(1, g, 1, pick[g], part)
 
+    for r in (1, 2, 3):
+        y_sum(r).wait_recv()
+    total = ys[2 * ypar + a].astype(F32)
+    for r in range(3):
+        total = total + y_in[r].astype(F32)
+    dx_v[...] = total.astype(BF16)
+    put_dx.start()
+
     wait_own(0)
     for g in range(2):
         rs(0, g, 1, FULL, 0).wait_recv()
-    dw = own_o[...].astype(F32) + rin_o[0].astype(F32) + lin_o[0].astype(F32)
-    dwout_out[...] = dw.T
 
     wait_own(1)
     for part, pick in ((1, seconds), (0, firsts)):
         for g in range(2):
             rs(1, g, 1, pick[g], part).wait_recv()
-    dwin_out[...] = own_i[...].astype(F32) + rin_i[0].astype(F32) + lin_i[0].astype(F32)
 
     @pl.when(jnp.logical_not(same))
     def _():
@@ -458,8 +478,16 @@
         for e in (2, 1):
             rs(1, g, e, seconds[g], 1).wait_send()
             rs(1, g, e, firsts[g], 0).wait_send()
-    for r, q in plane:
-        dx_cp(r, q).wait_send()
+    for r in (1, 2, 3):
+        x_sum(r).wait_send()
+        y_sum(r).wait_send()
+    put_dx.wait()
+
+
+def finish(dx_ref, in_ref, out_ref, dx_out, dwin_out, dwout_out):
+    dx_out[...] = dx_ref[...]
+    for ref, out in ((in_ref, dwin_out), (out_ref, dwout_out)):
+        out[...] = ref[0].astype(F32) + ref[1].astype(F32) + ref[2].astype(F32)
 
 
 def per_device(inputs, upstream, w_in, bias_in, w_out):
@@ -471,20 +499,19 @@
     ring = (NZ,) + shard
     acc = (2, ROWS, FC)
     turned = (NZ, 2, SH, ROWS)
-    return pl.pallas_call(
+    dx, parts_i, parts_o = pl.pallas_call(
         lambda *refs: kernel(scale, *refs),
         out_shape=(
-            jax.ShapeDtypeStruct((ROWS, SH), BF16),
-            jax.ShapeDtypeStruct((SH, FC), F32),
-            jax.ShapeDtypeStruct((FC, SH), F32),
+            jax.ShapeDtypeStruct((SH, ROWS), BF16),
+            jax.ShapeDtypeStruct((3,) + shard, BF16),
+            jax.ShapeDtypeStruct((3,) + shard, BF16),
         ),
         in_specs=[any_space, any_space, any_space, any_space, vmem],
-        out_specs=(vmem, vmem, vmem),
+        out_specs=(any_space, any_space, any_space),
         scratch_shapes=[
+            pltpu.VMEM((SH, ROWS), BF16),
             pltpu.VMEM((rows, width), BF16),
             pltpu.VMEM((rows, width), BF16),
-            pltpu.VMEM((FC, SH), BF16),
-            pltpu.VMEM(shard, BF16),
             pltpu.VMEM(turned, BF16),
             pltpu.VMEM(turned, BF16),
             pltpu.VMEM(ring, BF16),
@@ -498,16 +525,16 @@
             pltpu.VMEM(acc, F32),
             pltpu.VMEM(ring, BF16),
             pltpu.VMEM(ring, BF16),
-            pltpu.VMEM((4,) + shard, BF16),
-            pltpu.VMEM((4,) + shard, BF16),
-            pltpu.VMEM((4,) + shard, BF16),
-            pltpu.VMEM((4,) + shard, BF16),
-            pltpu.VMEM(shard, BF16),
-            pltpu.VMEM(shard, BF16),
-            pltpu.VMEM(turned, BF16),
-            pltpu.VMEM((16, SH, ROWS), BF16),
+            pltpu.VMEM((3,) + shard, BF16),
+            pltpu.VMEM((3,) + shard, BF16),
+            pltpu.VMEM((3,) + shard, BF16),
+            pltpu.VMEM((3,) + shard, BF16),
+            pltpu.VMEM((4, 4, SH, ROWS), BF16),
+            pltpu.VMEM((3, 4, SH, ROWS), BF16),
+            pltpu.VMEM((4, SH, ROWS), BF16),
+            pltpu.VMEM((3, SH, ROWS), BF16),
             pltpu.VMEM((2, 8, FC), F32),
-            pltpu.SemaphoreType.DMA((4,)),
+            pltpu.SemaphoreType.DMA((5,)),
             pltpu.SemaphoreType.DMA((2,)),
             pltpu.SemaphoreType.DMA((2,)),
             pltpu.SemaphoreType.DMA((32,)),
@@ -520,13 +547,29 @@
             pltpu.SemaphoreType.DMA((32,)),
             pltpu.SemaphoreType.DMA((4,)),
             pltpu.SemaphoreType.DMA((4,)),
-            pltpu.SemaphoreType.DMA((16,)),
-            pltpu.SemaphoreType.DMA((16,)),
+            pltpu.SemaphoreType.DMA((6,)),
+            pltpu.SemaphoreType.DMA((6,)),
         ],
         compiler_params=pltpu.CompilerParams(
             collective_id=0, has_side_effects=True, vmem_limit_bytes=60 * 1024 * 1024
         ),
-    )(inputs, upstream, w_in, w_out, bias_in.reshape(1, -1))
+    )(inputs, upstream, w_in, w_out.T, bias_in)
+    steps = 4
+    part_spec = pl.BlockSpec((3, SH // steps, FC), lambda i: (0, i, 0))
+    dx_spec = pl.BlockSpec((SH // steps, ROWS), lambda i: (i, 0))
+    dw_spec = pl.BlockSpec((SH // steps, FC), lambda i: (i, 0))
+    dx, dwin, dwout = pl.pallas_call(
+        finish,
+        grid=(steps,),
+        out_shape=(
+            jax.ShapeDtypeStruct((SH, ROWS), BF16),
+            jax.ShapeDtypeStruct(shard, F32),
+            jax.ShapeDtypeStruct(shard, F32),
+        ),
+        in_specs=[dx_spec, part_spec, part_spec],
+        out_specs=(dx_spec, dw_spec, dw_spec),
+    )(dx, parts_i, parts_o)
+    return dx.T, dwin, dwout.T
 
 
 def solution(mesh):

time: 163 us -> 147 us (0.902)
  the two profiles are of different devices: /device:TPU:45 before, /device:TPU:1 now
where the time goes in v2:
time: 147 us; the launch traced here: 145 us
  Pallas kernels  144 us (98%)
    pallas_call x1, Pallas kernels, per_device(): pl.pallas_call(lambda *refs: kernel(scale, *refs), out_shape=(jax.ShapeDt...  140 us
    pallas_call x1, Pallas kernels, per_device(): pl.pallas_call(finish, grid=(steps,), out_shape=(jax.ShapeDtypeStruct((SH...  3.8 us

profile of v2, /device:TPU:1, one launch (start us, length us, event | category | flops | bytes accessed | tf_op | source)
XLA Modules:
  0.0 144.6 jit_solution(3342702418306578072)
XLA Ops:
  0.6 140.2 %shard_map.76 = (bf16[320,256]{1,0:T(8,128)(2,1)}, bf16[3,320,640]{2,1,0:T(8,128)(2,1)}, bf16[3,320,640]{2,1,0:T(8,128)(2,1)}) custom-call(bf16[256,5120]{1,0:T(8,128)(2,1)} %refs_0_.1, bf16[256,5120]{1,0:T(8,128)(2,1)} %refs_1_.1, bf16[320,640]{1,0:T(8,128)(2,1)} %refs_2_.1, bf16[320,640]{1,0:T(8,128)(2,1)} %bitcast.3, bf16[640]{0:T(1024)(128)(2,1)} %refs_4_.1), custom_call_target="tpu_custom_call" | custom-call | tf_op jit(solution)/shard_map/pallas_call | solution.py:502
  140.8 3.8 %shard_map.77 = (bf16[320,256]{1,0:T(8,128)(2,1)}, f32[320,640]{1,0:T(8,128)}, f32[320,640]{1,0:T(8,128)}) custom-call(bf16[320,256]{1,0:T(8,128)(2,1)} %get-tuple-element.9.dx_ref, bf16[3,320,640]{2,1,0:T(8,128)(2,1)} %get-tuple-element.10.in_ref, bf16[3,320,640]{2,1,0:T(8,128)(2,1)} %get-tuple-element.11.out_ref), custom_call_target="tpu_custom_call" | custom-call | tf_op jit(solution)/shard_map/pallas_call | solution.py:561

commit v3 on v2

v3 whole, which is shorter than its diff:
```python
import math

import jax
import jax.numpy as jnp
from jax import lax
from jax.experimental import pallas as pl
from jax.experimental.pallas import tpu as pltpu
from jax.sharding import PartitionSpec as P

MESH = pl.DeviceIdType.MESH
ROOT_HALF = 0.7071067811865476
INV_ROOT_TWO_PI = 0.3989422804014327
BF16 = jnp.bfloat16
F32 = jnp.float32

NZ = 8
NT = 8
ROWS = 256
SH = 320
HF = SH // 2
FC = 640
PARTS = (pl.ds(0, HF), pl.ds(HF, HF))

TN = (((0,), (0,)), ((), ()))
NN = (((1,), (0,)), ((), ()))
NT_DIMS = (((1,), (1,)), ((), ()))


def dot(lhs, rhs, dims):
    return lax.dot_general(lhs, rhs, dims, preferred_element_type=F32)


def kernel(
    scale, x_hbm, dy_hbm, win_hbm, wout_hbm, bias_ref,
    dx_out, parts_i, parts_o,
    dx_v, xv, dyv, xt, dyt, wi, wo,
    pre, pre_in, act, ga, ga_in, gp, slope,
    term_o, term_i, rin_o, rin_i, lin_o, lin_i,
    dxa, dxb, sum_a, sum_b, in_a, in_b, last_a, last_b, turn_v, bias_in,
    ld_sem, sw_s, sw_r, ag_s, ag_r, ex_s, ex_r, core_s, core_r,
    rs_s, rs_r, own_s, own_r, dx_s, dx_r,
):
    dp = lax.axis_index("dp")
    tn = lax.axis_index("tensor")
    z, a = lax.div(dp, 2), lax.rem(dp, 2)
    t2, b = lax.div(tn, 2), lax.rem(tn, 2)
    x_, ypar = lax.div(t2, 2), lax.rem(t2, 2)
    y_ = 2 * a + ypar
    xpar = lax.rem(x_, 2)
    same = a == b
    differ = a != b
    zr, zl = lax.rem(z + 1, NZ), lax.rem(z + NZ - 1, NZ)

    def dev(z_, t_, a_, b_):
        return {"dp": 2 * z_ + a_, "tensor": 2 * t_ + b_}

    right, left = dev(zr, t2, a, b), dev(zl, t2, a, b)
    other_core = dev(z, t2, a, 1 - b)
    y_side = dev(z, t2 + 1 - 2 * ypar, 1 - a, b)
    x_side = dev(z, t2 + 2 - 4 * xpar, a, b)

    def x_peer(r):
        return lax.rem(x_ + r, 4)

    def y_peer(r):
        yy = lax.rem(y_ + r, 4)
        return lax.rem(yy, 2), lax.div(yy, 2)

    def x_dev(r):
        return dev(z, 2 * x_peer(r) + ypar, a, b)

    def y_dev(r):
        yl, ah = y_peer(r)
        return dev(z, 2 * x_ + yl, ah, b)

    def rc(src, dst, ss, rs, to):
        return pltpu.make_async_remote_copy(
            src_ref=src, dst_ref=dst, send_sem=ss, recv_sem=rs, device_id=to, device_id_type=MESH
        )

    def part_rows(p):
        if isinstance(p, int):
            return PARTS[p]
        return pl.ds(pl.multiple_of(p * HF, HF), HF)

    hbm = (win_hbm, wout_hbm)
    weights = (wi, wo)
    here = part_rows(b)

    def ld_w(w):
        return pltpu.make_async_copy(hbm[w].at[here], weights[w].at[0, part_rows(a)], ld_sem.at[2 + w])

    ld_x = pltpu.make_async_copy(x_hbm, xv, ld_sem.at[0])
    ld_dy = pltpu.make_async_copy(dy_hbm, dyv, ld_sem.at[1])
    put_dx = pltpu.make_async_copy(dx_v, dx_out, ld_sem.at[4])

    @pl.when(same)
    def _():
        ld_w(0).start()
        ld_w(1).start()

    ld_x.start()
    ld_dy.start()

    barrier = pltpu.get_barrier_semaphore()

    def greet(to):
        pl.semaphore_signal(barrier, inc=1, device_id=to, device_id_type=MESH)

    for z_ in (zr, zl):
        for i in range(4):
            greet(dev(z_, t2, i // 2, i % 2))
    greet(other_core)
    greet(dev(z, t2, 1 - a, b))
    greet(dev(z, t2, 1 - a, 1 - b))
    for r in (1, 2, 3):
        greet(x_dev(r))
    greet(y_dev(1))
    greet(y_dev(3))
    pl.semaphore_wait(barrier, 16)

    def to_twin(w):
        rows = part_rows(a)
        return rc(hbm[w].at[part_rows(1 - b)], weights[w].at[0, rows], sw_s.at[2 * w], sw_r.at[2 * w], other_core)

    def to_chip(w, h):
        rows = part_rows(a)
        return rc(
            hbm[w].at[part_rows(h)], weights[w].at[0, rows], sw_s.at[2 * w + h], sw_r.at[2 * w + 1], dev(z, t2, b, h)
        )

    def from_twin(w):
        return rc(hbm[w].at[here], weights[w].at[0, part_rows(a)], sw_s.at[2 * w], sw_r.at[2 * w], other_core)

    def from_chip(w):
        return rc(hbm[w].at[here], weights[w].at[0, part_rows(1 - a)], sw_s.at[2 * w], sw_r.at[2 * w + 1], other_core)

    @pl.when(same)
    def _():
        to_twin(0).start()
        to_twin(1).start()

    @pl.when(differ)
    def _():
        for w in range(2):
            for h in range(2):
                to_chip(w, h).start()

    def ag(w, g, s, part):
        buf, rows = weights[w], part_rows(part)
        if g == 0:
            src, dst, to = s - 1, s, right
        else:
            src, dst, to = (NZ + 1 - s) % NZ, NZ - s, left
        i = ((w * 2 + g) * 4 + s - 1) * 2 + part
        return rc(buf.at[src, rows], buf.at[dst, rows], ag_s.at[i], ag_r.at[i], to)

    def send_first(w, part):
        for g in range(2):
            ag(w, g, 1, part).start()

    for w in range(2):
        @pl.when(same)
        def _():
            ld_w(w).wait()

        @pl.when(differ)
        def _():
            from_twin(w).wait_recv()

        send_first(w, a)

    bias_in[0] = jnp.broadcast_to(bias_ref[...].astype(F32)[None, :], (8, FC))
    bias_cp = rc(bias_in.at[0], bias_in.at[1], core_s.at[2], core_r.at[2], other_core)
    bias_cp.start()

    pairs = ((0, 1), (7, 2), (6, 3), (5, 4))

    def mine(i):
        p, q = pairs[i]
        return p + (q - p) * xpar

    def theirs(i):
        p, q = pairs[i]
        return q + (p - q) * xpar

    def turn(src, dst, d):
        k = lax.rem(z + NZ - d, NZ)
        v = src[:, pl.ds(pl.multiple_of(k * 2 * SH, 128), 2 * SH)].T
        first = b == 0
        dst[d, a, PARTS[0]] = jnp.where(first, v[:HF], v[HF:SH])
        dst[d, a, PARTS[1]] = jnp.where(first, v[SH : SH + HF], v[SH + HF :])

    rows_t = (xt, dyt)

    def ex_y(w, i):
        buf, d, m = rows_t[w], mine(i), w * 8 + i
        return rc(buf.at[d, a], buf.at[d, a], ex_s.at[m], ex_r.at[m], y_side)

    def ex_y_in(w, i):
        buf, d, m = rows_t[w], mine(i), w * 8 + i
        return rc(buf.at[d, 1 - a], buf.at[d, 1 - a], ex_s.at[m], ex_r.at[m], y_side)

    def ex_x(w, i):
        buf, d, m = rows_t[w], mine(i), w * 8 + 4 + i
        return rc(buf.at[d, 1 - a], buf.at[d, 1 - a], ex_s.at[m], ex_r.at[m], x_side)

    def ex_x_in(w, i):
        buf, d, m = rows_t[w], theirs(i), w * 8 + 4 + i
        return rc(buf.at[d, 1 - a], buf.at[d, 1 - a], ex_s.at[m], ex_r.at[m], x_side)

    ld_x.wait()
    for d in range(NZ):
        turn(xv, xt, d)

    for w in range(2):
        from_chip(w).wait_recv()
        send_first(w, 1 - a)

    for i in range(4):
        ex_y(0, i).start()
    ld_dy.wait()
    for d in range(NZ):
        turn(dyv, dyt, d)
    for i in range(4):
        ex_y(1, i).start()

    def pass_on(w, i):
        ex_y_in(w, i).wait_recv()
        ex_x(w, i).start()

    def step(w, s, part):
        for g in range(2):
            ag(w, g, s, part).wait_recv()
            ag(w, g, s + 1, part).start()

    def accumulate(acc, src, w, slots, first=False):
        n = len(slots)

        def body(i, carry):
            j, h = lax.div(i, 2), lax.rem(i, 2)
            d = slots[0] if n == 1 else slots[0] + j * (slots[1] - slots[0])
            acc[h] += dot(src[d, h], w[d], TN)
            return carry

        if first:
            acc[...] = jnp.zeros_like(acc)
        lax.fori_loop(0, 2 * n, body, 0)

    firsts = (0, 1)
    seconds = (1, 0)

    for w in range(2):
        step(w, 1, a)
        step(w, 1, 1 - a)
    for i in range(2):
        pass_on(0, i)
    step(0, 2, a)
    for i in range(2, 4):
        pass_on(0, i)
    step(0, 2, 1 - a)
    for i in range(2):
        ex_x_in(0, i).wait_recv()
    accumulate(pre, xt, wi, (0,), True)
    accumulate(pre, xt, wi, (1, 7))
    pass_on(1, 0)
    for i in range(2, 4):
        ex_x_in(0, i).wait_recv()
    accumulate(pre, xt, wi, (2, 6))
    pass_on(1, 1)
    for part in (a, 1 - a):
        for g in range(2):
            ag(1, g, 2, part).wait_recv()
    pass_on(1, 2)
    for g in range(2):
        ag(0, g, 3, firsts[g]).wait_recv()
        ag(0, g, 4, firsts[g]).start()
    for pick in (firsts, seconds):
        for g in range(2):
            ag(1, g, 3, pick[g]).start()
    pass_on(1, 3)
    for g in range(2):
        ag(0, g, 3, seconds[g]).wait_recv()
    accumulate(pre, xt, wi, (3, 5))
    for g in range(2):
        ag(0, g, 4, firsts[g]).wait_recv()
    accumulate(pre, xt, wi, (4,))
    pre_cp = rc(pre, pre_in, core_s.at[0], core_r.at[0], other_core)
    pre_cp.start()
    for i in range(4):
        ex_x_in(1, i).wait_recv()
    accumulate(ga, dyt, wo, (0,), True)
    accumulate(ga, dyt, wo, (1, 7))
    for g in range(2):
        ag(1, g, 3, firsts[g]).wait_recv()
        ag(1, g, 4, firsts[g]).start()
    accumulate(ga, dyt, wo, (2, 6))
    bias_cp.wait_recv()
    bias = jnp.where(same, bias_in[0], bias_in[1])[0:1]
    pre_cp.wait_recv()

    def gelu(i, carry):
        h, rows = lax.div(i, 8), pl.ds(pl.multiple_of(lax.rem(i, 8) * 32, 32), 32)
        v = pre[h, rows] + pre_in[h, rows] + bias
        cdf = 0.5 * (1.0 + lax.erf(v * ROOT_HALF))
        act[h, rows] = (v * cdf).astype(BF16)
        slope[h, rows] = cdf + v * jnp.exp(-0.5 * v * v) * INV_ROOT_TWO_PI
        return carry

    lax.fori_loop(0, 16, gelu, 0)

    terms, rins, lins, ends = (term_o, term_i), (rin_o, rin_i), (lin_o, lin_i), (parts_o, parts_i)

    def make_terms(w, lo, hi):
        src, val, out = (dyt, xt)[w], (act, gp)[w], terms[w]

        def body(i, carry):
            d = lax.rem(4 + lax.div(i + 1, 2) * (2 * lax.rem(i, 2) - 1) + NZ, NZ)
            total = dot(src[d, 0], val[0], NN) + dot(src[d, 1], val[1], NN)
            out[d] = (total * scale).astype(BF16)
            return carry

        lax.fori_loop(lo, hi, body, 0)

    def rs(w, g, e, part):
        rows = part_rows(part)
        src = terms[w].at[NZ - e if g == 0 else e, rows]
        i = (w * 2 + g) * 4 + e - 1
        if e > 1:
            dst, to, m = (rins, lins)[g][w].at[e - 2, rows], (right, left)[g], 2 * i + part
        else:
            dst, to, m = ends[w].at[1 + g, here], dev((zr, zl)[g], t2, part, a), 2 * i + b
        return rc(src, dst, rs_s.at[2 * i + part], rs_r.at[m], to)

    def rs_end(w, g, h):
        rows, m = PARTS[h], 2 * ((w * 2 + g) * 4) + h
        return rc(terms[w].at[0, rows], ends[w].at[1 + g, rows], rs_s.at[m], rs_r.at[m], right)

    def hop(w, g, e, part):
        rs(w, g, e + 1, part).wait_recv()
        d, rows = NZ - e if g == 0 else e, part_rows(part)
        buf, came = terms[w], (rins, lins)[g][w]
        buf[d, rows] = (buf[d, rows].astype(F32) + came[e - 1, rows].astype(F32)).astype(BF16)
        rs(w, g, e, part).start()

    def own_copy(w, p):
        return rc(
            terms[w].at[0, PARTS[p]], ends[w].at[0, here], own_s.at[2 * w + p], own_r.at[2 * w + b], dev(z, t2, p, a)
        )

    def own_local(w, p):
        return pltpu.make_async_copy(terms[w].at[0, PARTS[p]], ends[w].at[0, here], own_s.at[2 * w + p])

    def own_end(w, h):
        return rc(terms[w].at[0, PARTS[h]], ends[w].at[0, PARTS[h]], own_s.at[0], own_r.at[2 * w + h], right)

    def send_own(w):
        for p in range(2):
            stays = same & (a == p)

            @pl.when(stays)
            def _():
                own_local(w, p).start()

            @pl.when(jnp.logical_not(stays))
            def _():
                own_copy(w, p).start()

    def wait_own(w):
        for p in range(2):
            stays = same & (a == p)

            @pl.when(stays)
            def _():
                own_local(w, p).wait()

            @pl.when(jnp.logical_not(stays))
            def _():
                own_copy(w, p).wait_send()

        for h in range(2):
            @pl.when(jnp.logical_not(same & (b == h)))
            def _():
                own_end(w, h).wait_recv()

    make_terms(0, 0, 3)
    for g in range(2):
        rs(0, g, 4, firsts[g]).start()
    for g in range(2):
        rs(0, g, 3, seconds[g]).start()
    for g in range(2):
        ag(1, g, 3, seconds[g]).wait_recv()
    accumulate(ga, dyt, wo, (3, 5))
    for g in range(2):
        ag(1, g, 4, firsts[g]).wait_recv()
    accumulate(ga, dyt, wo, (4,))
    ga_cp = rc(ga, ga_in, core_s.at[1], core_r.at[1], other_core)
    ga_cp.start()
    make_terms(0, 3, 8)
    for g in range(2):
        hop(0, g, 3, firsts[g])
    send_own(0)
    ga_cp.wait_recv()

    def grad(i, carry):
        h, rows = lax.div(i, 8), pl.ds(pl.multiple_of(lax.rem(i, 8) * 32, 32), 32)
        gp[h, rows] = ((ga[h, rows] + ga_in[h, rows]) * slope[h, rows]).astype(BF16)
        return carry

    lax.fori_loop(0, 16, grad, 0)
    make_terms(1, 0, 3)
    for g in range(2):
        rs(1, g, 4, firsts[g]).start()
    for g in range(2):
        rs(1, g, 3, seconds[g]).start()

    def dx_body(i, carry):
        k, h = lax.div(i, 2), lax.rem(i, 2)
        d = lax.rem(z + NZ - k, NZ)
        v = dot(wi[d], gp[h], NT_DIMS).astype(BF16)
        xx, yy = lax.div(k, 2), 2 * lax.rem(k, 2) + h
        dxa[xx, yy] = v[:HF]
        dxb[yy, xx] = v[HF:]
        return carry

    lax.fori_loop(0, 16, dx_body, 0)
    yy_ = 2 * ypar + a

    def y_index(r):
        yl, ah = y_peer(r)
        return 2 * yl + ah

    def first_a(r):
        return rc(dxa.at[x_peer(r)], in_a.at[r - 1], dx_s.at[r - 1], dx_r.at[r - 1], x_dev(r))

    def first_b(r):
        return rc(dxb.at[y_index(r)], in_b.at[r - 1], dx_s.at[r + 2], dx_r.at[r + 2], y_dev(r))

    def second_a(r):
        return rc(sum_a.at[y_index(r)], last_a.at[r - 1], dx_s.at[r + 5], dx_r.at[r + 5], y_dev(r))

    def second_b(r):
        return rc(sum_b.at[x_peer(r)], last_b.at[r - 1], dx_s.at[r + 8], dx_r.at[r + 8], x_dev(r))

    for r in (1, 2, 3):
        first_a(r).start()
        first_b(r).start()

    make_terms(1, 3, 8)
    send_own(1)
    for pick in (seconds, firsts):
        for g in range(2):
            hop(0, g, 2, pick[g])
    for g in range(2):
        hop(1, g, 3, firsts[g])
    for pick in (seconds, firsts):
        for g in range(2):
            hop(0, g, 1, pick[g])

    for r in (1, 2, 3):
        first_a(r).wait_recv()
        first_b(r).wait_recv()

    def sum_body(i, carry):
        total_a, total_b = dxa[x_, i].astype(F32), dxb[yy_, i].astype(F32)
        for r in range(3):
            total_a = total_a + in_a[r, i].astype(F32)
            total_b = total_b + in_b[r, i].astype(F32)
        sum_a[i], sum_b[i] = total_a.astype(BF16), total_b.astype(BF16)
        return carry

    lax.fori_loop(0, 4, sum_body, 0)
    for r in (1, 2, 3):
        second_a(r).start()
        second_b(r).start()

    for pick in (seconds, firsts):
        for g in range(2):
            hop(1, g, 2, pick[g])

    for pick in (seconds, firsts):
        for g in range(2):
            hop(1, g, 1, pick[g])

    for r in (1, 2, 3):
        second_a(r).wait_recv()
        second_b(r).wait_recv()
    total_a, total_b = sum_a[yy_].astype(F32), sum_b[x_].astype(F32)
    for r in range(3):
        total_a = total_a + last_a[r].astype(F32)
        total_b = total_b + last_b[r].astype(F32)
    total_a, total_b = total_a.astype(BF16), total_b.astype(BF16)
    dx_v[here] = jnp.where(b == 0, total_a, total_b)
    turn_v[...] = jnp.where(b == 0, total_b, total_a)
    dx_cp = rc(turn_v, dx_v.at[here], core_s.at[3], core_r.at[3], other_core)
    dx_cp.start()

    rc(turn_v, dx_v.at[part_rows(1 - b)], core_s.at[3], core_r.at[3], other_core).wait_recv()
    put_dx.start()

    for w in range(2):
        wait_own(w)
        for g in range(2):
            for h in range(2):
                rs_end(w, g, h).wait_recv()

    @pl.when(same)
    def _():
        to_twin(0).wait_send()
        to_twin(1).wait_send()

    @pl.when(differ)
    def _():
        for w in range(2):
            for h in range(2):
                to_chip(w, h).wait_send()

    for w in range(2):
        for g in range(2):
            for s in (1, 2, 3):
                for part in range(2):
                    ag(w, g, s, part).wait_send()
            ag(w, g, 4, firsts[g]).wait_send()
        for i in range(4):
            ex_y(w, i).wait_send()
            ex_x(w, i).wait_send()
    for cp in (bias_cp, pre_cp, ga_cp, dx_cp):
        cp.wait_send()
    for w in range(2):
        for g in range(2):
            rs(w, g, 4, firsts[g]).wait_send()
            for e in (3, 2, 1):
                for part in range(2):
                    rs(w, g, e, part).wait_send()
    for r in (1, 2, 3):
        for cp in (first_a(r), first_b(r), second_a(r), second_b(r)):
            cp.wait_send()
    put_dx.wait()


def finish(dx_ref, in_ref, out_ref, dx_out, dwin_out, dwout_out):
    dx_out[...] = dx_ref[...]
    for ref, out in ((in_ref, dwin_out), (out_ref, dwout_out)):
        out[...] = ref[0].astype(F32) + ref[1].astype(F32) + ref[2].astype(F32)


def per_device(inputs, upstream, w_in, bias_in, w_out):
    rows, width = inputs.shape
    scale = 1.0 / math.sqrt(rows * lax.axis_size("dp"))
    any_space = pl.BlockSpec(memory_space=pl.ANY)
    vmem = pl.BlockSpec(memory_space=pltpu.VMEM)
    shard = (SH, FC)
    ring = (NZ,) + shard
    acc = (2, ROWS, FC)
    turned = (NZ, 2, SH, ROWS)
    dx, parts_i, parts_o = pl.pallas_call(
        lambda *refs: kernel(scale, *refs),
        out_shape=(
            jax.ShapeDtypeStruct((SH, ROWS), BF16),
            jax.ShapeDtypeStruct((3,) + shard, BF16),
            jax.ShapeDtypeStruct((3,) + shard, BF16),
        ),
        in_specs=[any_space, any_space, any_space, any_space, vmem],
        out_specs=(any_space, any_space, any_space),
        scratch_shapes=[
            pltpu.VMEM((SH, ROWS), BF16),
            pltpu.VMEM((rows, width), BF16),
            pltpu.VMEM((rows, width), BF16),
            pltpu.VMEM(turned, BF16),
            pltpu.VMEM(turned, BF16),
            pltpu.VMEM(ring, BF16),
            pltpu.VMEM(ring, BF16),
            pltpu.VMEM(acc, F32),
            pltpu.VMEM(acc, F32),
            pltpu.VMEM(acc, BF16),
            pltpu.VMEM(acc, F32),
            pltpu.VMEM(acc, F32),
            pltpu.VMEM(acc, BF16),
            pltpu.VMEM(acc, F32),
            pltpu.VMEM(ring, BF16),
            pltpu.VMEM(ring, BF16),
            pltpu.VMEM((3,) + shard, BF16),
            pltpu.VMEM((3,) + shard, BF16),
            pltpu.VMEM((3,) + shard, BF16),
            pltpu.VMEM((3,) + shard, BF16),
            pltpu.VMEM((4, 4, HF, ROWS), BF16),
            pltpu.VMEM((4, 4, HF, ROWS), BF16),
            pltpu.VMEM((4, HF, ROWS), BF16),
            pltpu.VMEM((4, HF, ROWS), BF16),
            pltpu.VMEM((3, 4, HF, ROWS), BF16),
            pltpu.VMEM((3, 4, HF, ROWS), BF16),
            pltpu.VMEM((3, HF, ROWS), BF16),
            pltpu.VMEM((3, HF, ROWS), BF16),
            pltpu.VMEM((HF, ROWS), BF16),
            pltpu.VMEM((2, 8, FC), F32),
            pltpu.SemaphoreType.DMA((5,)),
            pltpu.SemaphoreType.DMA((4,)),
            pltpu.SemaphoreType.DMA((4,)),
            pltpu.SemaphoreType.DMA((32,)),
            pltpu.SemaphoreType.DMA((32,)),
            pltpu.SemaphoreType.DMA((16,)),
            pltpu.SemaphoreType.DMA((16,)),
            pltpu.SemaphoreType.DMA((4,)),
            pltpu.SemaphoreType.DMA((4,)),
            pltpu.SemaphoreType.DMA((32,)),
            pltpu.SemaphoreType.DMA((32,)),
            pltpu.SemaphoreType.DMA((4,)),
            pltpu.SemaphoreType.DMA((4,)),
            pltpu.SemaphoreType.DMA((12,)),
            pltpu.SemaphoreType.DMA((12,)),
        ],
        compiler_params=pltpu.CompilerParams(
            collective_id=0, has_side_effects=True, vmem_limit_bytes=60 * 1024 * 1024
        ),
    )(inputs, upstream, w_in, w_out.T, bias_in)
    steps = 2
    part_spec = pl.BlockSpec((3, SH // steps, FC), lambda i: (0, i, 0))
    dx_spec = pl.BlockSpec((SH // steps, ROWS), lambda i: (i, 0))
    dw_spec = pl.BlockSpec((SH // steps, FC), lambda i: (i, 0))
    dx, dwin, dwout = pl.pallas_call(
        finish,
        grid=(steps,),
        out_shape=(
            jax.ShapeDtypeStruct((SH, ROWS), BF16),
            jax.ShapeDtypeStruct(shard, F32),
            jax.ShapeDtypeStruct(shard, F32),
        ),
        in_specs=[dx_spec, part_spec, part_spec],
        out_specs=(dx_spec, dw_spec, dw_spec),
    )(dx, parts_i, parts_o)
    return dx.T, dwin, dwout.T


def solution(mesh):
    placed = (P("dp", None), P("dp", None), P("dp", "tensor"), P("tensor"), P("tensor", "dp"))
    return jax.shard_map(
        per_device,
        mesh=mesh,
        in_specs=placed,
        out_specs=(P("dp", "tensor"), P("dp", "tensor"), P("tensor", "dp")),
        check_vma=False,
    )
```

time: 147 us -> 143 us (0.973); the launches traced: 145 us -> 142 us
  Pallas kernels: 144 us -> 142 us
where the time goes in v3:
time: 143 us; the launch traced here: 142 us
  Pallas kernels  142 us (99%)
    pallas_call x1, Pallas kernels, per_device(): pl.pallas_call(lambda *refs: kernel(scale, *refs), out_shape=(jax.ShapeDt...  139 us

profile of v3, /device:TPU:1, one launch (start us, length us, event | category | flops | bytes accessed | tf_op | source)
XLA Modules:
  0.0 142.5 jit_solution(3464368150249195138)
XLA Ops:
  0.6 139.1 %shard_map.76 = (bf16[320,256]{1,0:T(8,128)(2,1)}, bf16[3,320,640]{2,1,0:T(8,128)(2,1)}, bf16[3,320,640]{2,1,0:T(8,128)(2,1)}) custom-call(bf16[256,5120]{1,0:T(8,128)(2,1)} %refs_0_.1, bf16[256,5120]{1,0:T(8,128)(2,1)} %refs_1_.1, bf16[320,640]{1,0:T(8,128)(2,1)} %refs_2_.1, bf16[320,640]{1,0:T(8,128)(2,1)} %bitcast.3, bf16[640]{0:T(1024)(128)(2,1)} %refs_4_.1), custom_call_target="tpu_custom_call" | custom-call | tf_op jit(solution)/shard_map/pallas_call | solution.py:556
  139.8 2.7 %shard_map.77 = (bf16[320,256]{1,0:T(8,128)(2,1)}, f32[320,640]{1,0:T(8,128)}, f32[320,640]{1,0:T(8,128)}) custom-call(bf16[320,256]{1,0:T(8,128)(2,1)} %get-tuple-element.9.dx_ref, bf16[3,320,640]{2,1,0:T(8,128)(2,1)} %get-tuple-element.10.in_ref, bf16[3,320,640]{2,1,0:T(8,128)(2,1)} %get-tuple-element.11.out_ref), custom_call_target="tpu_custom_call" | custom-call | tf_op jit(solution)/shard_map/pallas_call | solution.py:620

commit v4 on v3

--- a/solution.py
+++ b/solution.py
@@ -108,8 +108,8 @@
         pl.semaphore_signal(barrier, inc=1, device_id=to, device_id_type=MESH)
 
     for z_ in (zr, zl):
-        for i in range(4):
-            greet(dev(z_, t2, i // 2, i % 2))
+        greet(dev(z_, t2, a, b))
+        greet(dev(z_, t2, a, 1 - b))
     greet(other_core)
     greet(dev(z, t2, 1 - a, b))
     greet(dev(z, t2, 1 - a, 1 - b))
@@ -117,7 +117,7 @@
         greet(x_dev(r))
     greet(y_dev(1))
     greet(y_dev(3))
-    pl.semaphore_wait(barrier, 16)
+    pl.semaphore_wait(barrier, 12)
 
     def to_twin(w):
         rows = part_rows(a)
@@ -255,10 +255,14 @@
         step(w, 1, 1 - a)
     for i in range(2):
         pass_on(0, i)
-    step(0, 2, a)
+    for part in (a, 1 - a):
+        for g in range(2):
+            ag(0, g, 2, part).wait_recv()
+    for pick in (firsts, seconds):
+        for g in range(2):
+            ag(0, g, 3, pick[g]).start()
     for i in range(2, 4):
         pass_on(0, i)
-    step(0, 2, 1 - a)
     for i in range(2):
         ex_x_in(0, i).wait_recv()
     accumulate(pre, xt, wi, (0,), True)
@@ -322,66 +326,74 @@
 
         lax.fori_loop(lo, hi, body, 0)
 
-    def rs(w, g, e, part):
+    def rs(w, g, e, part, last=False):
         rows = part_rows(part)
         src = terms[w].at[NZ - e if g == 0 else e, rows]
-        i = (w * 2 + g) * 4 + e - 1
-        if e > 1:
-            dst, to, m = (rins, lins)[g][w].at[e - 2, rows], (right, left)[g], 2 * i + part
-        else:
-            dst, to, m = ends[w].at[1 + g, here], dev((zr, zl)[g], t2, part, a), 2 * i + b
-        return rc(src, dst, rs_s.at[2 * i + part], rs_r.at[m], to)
-
-    def rs_end(w, g, h):
-        rows, m = PARTS[h], 2 * ((w * 2 + g) * 4) + h
-        return rc(terms[w].at[0, rows], ends[w].at[1 + g, rows], rs_s.at[m], rs_r.at[m], right)
-
-    def hop(w, g, e, part):
+        i = ((w * 2 + g) * 4 + e - 1) * 2 + part
+        if last:
+            m = 4 + (w * 2 + g) * 2 + b
+            return rc(src, ends[w].at[1 + g, here], rs_s.at[i], own_r.at[m], dev((zr, zl)[g], t2, a, a))
+        return rc(src, (rins, lins)[g][w].at[e - 1, rows], rs_s.at[i], rs_r.at[i], (right, left)[g])
+
+    def last_in(w, g, h):
+        m = 4 + (w * 2 + g) * 2 + h
+        return rc(terms[w].at[0, PARTS[h]], ends[w].at[1 + g, PARTS[h]], own_s.at[0], own_r.at[m], right)
+
+    def hop(w, g, e, part, last=False):
         rs(w, g, e + 1, part).wait_recv()
         d, rows = NZ - e if g == 0 else e, part_rows(part)
         buf, came = terms[w], (rins, lins)[g][w]
-        buf[d, rows] = (buf[d, rows].astype(F32) + came[e - 1, rows].astype(F32)).astype(BF16)
-        rs(w, g, e, part).start()
-
-    def own_copy(w, p):
+        buf[d, rows] = (buf[d, rows].astype(F32) + came[e, rows].astype(F32)).astype(BF16)
+        rs(w, g, e, part, last).start()
+
+    def end_copy(w, part):
+        m = 2 * w + part
         return rc(
-            terms[w].at[0, PARTS[p]], ends[w].at[0, here], own_s.at[2 * w + p], own_r.at[2 * w + b], dev(z, t2, p, a)
+            terms[w].at[0, part_rows(part)], ends[w].at[0, here], own_s.at[m], own_r.at[2 * w + b], dev(z, t2, part, a)
         )
 
-    def own_local(w, p):
-        return pltpu.make_async_copy(terms[w].at[0, PARTS[p]], ends[w].at[0, here], own_s.at[2 * w + p])
-
-    def own_end(w, h):
+    def end_local(w):
+        return pltpu.make_async_copy(terms[w].at[0, part_rows(a)], ends[w].at[0, here], own_s.at[2 * w + a])
+
+    def end_in(w, h):
         return rc(terms[w].at[0, PARTS[h]], ends[w].at[0, PARTS[h]], own_s.at[0], own_r.at[2 * w + h], right)
 
     def send_own(w):
-        for p in range(2):
-            stays = same & (a == p)
-
-            @pl.when(stays)
-            def _():
-                own_local(w, p).start()
-
-            @pl.when(jnp.logical_not(stays))
-            def _():
-                own_copy(w, p).start()
-
-    def wait_own(w):
-        for p in range(2):
-            stays = same & (a == p)
-
-            @pl.when(stays)
-            def _():
-                own_local(w, p).wait()
-
-            @pl.when(jnp.logical_not(stays))
-            def _():
-                own_copy(w, p).wait_send()
-
+        @pl.when(same)
+        def _():
+            end_local(w).start()
+
+        @pl.when(differ)
+        def _():
+            end_copy(w, a).start()
+
+    def send_sum(w):
+        rows = part_rows(1 - a)
+        for g in range(2):
+            rs(w, g, 1, 1 - a).wait_recv()
+        total = terms[w][0, rows].astype(F32)
+        for came in (rins[w], lins[w]):
+            total = total + came[0, rows].astype(F32)
+        terms[w][0, rows] = total.astype(BF16)
+        end_copy(w, 1 - a).start()
+
+    def wait_end(w):
+        @pl.when(same)
+        def _():
+            end_local(w).wait()
+            for g in range(2):
+                for h in range(2):
+                    last_in(w, g, h).wait_recv()
+
+        @pl.when(differ)
+        def _():
+            end_copy(w, a).wait_send()
+
+        end_copy(w, 1 - a).wait_send()
         for h in range(2):
             @pl.when(jnp.logical_not(same & (b == h)))
             def _():
-                own_end(w, h).wait_recv()
+                end_in(w, h).wait_recv()
 
     make_terms(0, 0, 3)
     for g in range(2):
@@ -448,14 +460,17 @@
 
     make_terms(1, 3, 8)
     send_own(1)
-    for pick in (seconds, firsts):
-        for g in range(2):
-            hop(0, g, 2, pick[g])
+    for part in (1 - a, a):
+        for g in range(2):
+            hop(0, g, 2, part)
     for g in range(2):
         hop(1, g, 3, firsts[g])
-    for pick in (seconds, firsts):
-        for g in range(2):
-            hop(0, g, 1, pick[g])
+    for g in range(2):
+        hop(1, g, 2, 1 - a)
+    for g in range(2):
+        hop(0, g, 1, 1 - a)
+    for g in range(2):
+        hop(1, g, 2, a)
 
     for r in (1, 2, 3):
         first_a(r).wait_recv()
@@ -474,13 +489,14 @@
         second_a(r).start()
         second_b(r).start()
 
-    for pick in (seconds, firsts):
-        for g in range(2):
-            hop(1, g, 2, pick[g])
-
-    for pick in (seconds, firsts):
-        for g in range(2):
-            hop(1, g, 1, pick[g])
+    for g in range(2):
+        hop(1, g, 1, 1 - a)
+    for g in range(2):
+        hop(0, g, 1, a, True)
+    send_sum(0)
+    for g in range(2):
+        hop(1, g, 1, a, True)
+    send_sum(1)
 
     for r in (1, 2, 3):
         second_a(r).wait_recv()
@@ -498,11 +514,6 @@
     rc(turn_v, dx_v.at[part_rows(1 - b)], core_s.at[3], core_r.at[3], other_core).wait_recv()
     put_dx.start()
 
-    for w in range(2):
-        wait_own(w)
-        for g in range(2):
-            for h in range(2):
-                rs_end(w, g, h).wait_recv()
 
     @pl.when(same)
     def _():
@@ -524,24 +535,38 @@
         for i in range(4):
             ex_y(w, i).wait_send()
             ex_x(w, i).wait_send()
-    for cp in (bias_cp, pre_cp, ga_cp, dx_cp):
+    for cp in (bias_cp, pre_cp, ga_cp):
         cp.wait_send()
     for w in range(2):
         for g in range(2):
             rs(w, g, 4, firsts[g]).wait_send()
-            for e in (3, 2, 1):
+            for e in (3, 2) if w else (3, 2, 1):
                 for part in range(2):
                     rs(w, g, e, part).wait_send()
     for r in (1, 2, 3):
         for cp in (first_a(r), first_b(r), second_a(r), second_b(r)):
             cp.wait_send()
+
+    wait_end(0)
+    wait_end(1)
+    for g in range(2):
+        for part in range(2):
+            rs(1, g, 1, part).wait_send()
+    dx_cp.wait_send()
     put_dx.wait()
 
 
 def finish(dx_ref, in_ref, out_ref, dx_out, dwin_out, dwout_out):
     dx_out[...] = dx_ref[...]
+    whole = lax.rem(lax.axis_index("dp"), 2) != lax.rem(lax.axis_index("tensor"), 2)
     for ref, out in ((in_ref, dwin_out), (out_ref, dwout_out)):
-        out[...] = ref[0].astype(F32) + ref[1].astype(F32) + ref[2].astype(F32)
+        @pl.when(whole)
+        def _():
+            out[...] = ref[0].astype(F32)
+
+        @pl.when(jnp.logical_not(whole))
+        def _():
+            out[...] = ref[0].astype(F32) + ref[1].astype(F32) + ref[2].astype(F32)
 
 
 def per_device(inputs, upstream, w_in, bias_in, w_out):
@@ -579,10 +604,10 @@
             pltpu.VMEM(acc, F32),
             pltpu.VMEM(ring, BF16),
             pltpu.VMEM(ring, BF16),
-            pltpu.VMEM((3,) + shard, BF16),
-            pltpu.VMEM((3,) + shard, BF16),
-            pltpu.VMEM((3,) + shard, BF16),
-            pltpu.VMEM((3,) + shard, BF16),
+            pltpu.VMEM((4,) + shard, BF16),
+            pltpu.VMEM((4,) + shard, BF16),
+            pltpu.VMEM((4,) + shard, BF16),
+            pltpu.VMEM((4,) + shard, BF16),
             pltpu.VMEM((4, 4, HF, ROWS), BF16),
             pltpu.VMEM((4, 4, HF, ROWS), BF16),
             pltpu.VMEM((4, HF, ROWS), BF16),
@@ -605,7 +630,7 @@
             pltpu.SemaphoreType.DMA((32,)),
             pltpu.SemaphoreType.DMA((32,)),
             pltpu.SemaphoreType.DMA((4,)),
-            pltpu.SemaphoreType.DMA((4,)),
+            pltpu.SemaphoreType.DMA((12,)),
             pltpu.SemaphoreType.DMA((12,)),
             pltpu.SemaphoreType.DMA((12,)),
         ],

time: 143 us -> 140 us (0.979)
  Pallas kernels: 142 us -> 139 us
    pallas_call x1, Pallas kernels: 139 us -> 137 us  [per_device(): pl.pallas_call(lambda *refs: kernel(scale, *refs), out_shape=(jax.ShapeDt...]
where the time goes in v4:
time: 140 us
  Pallas kernels  139 us (99%)
    pallas_call x1, Pallas kernels, per_device(): pl.pallas_call(lambda *refs: kernel(scale, *refs), out_shape=(jax.ShapeDt...  137 us

profile of v4, /device:TPU:1, one launch (start us, length us, event | category | flops | bytes accessed | tf_op | source)
XLA Modules:
  0.0 140.1 jit_solution(9793867981885544476)
XLA Ops:
  0.6 136.8 %shard_map.76 = (bf16[320,256]{1,0:T(8,128)(2,1)}, bf16[3,320,640]{2,1,0:T(8,128)(2,1)}, bf16[3,320,640]{2,1,0:T(8,128)(2,1)}) custom-call(bf16[256,5120]{1,0:T(8,128)(2,1)} %refs_0_.1, bf16[256,5120]{1,0:T(8,128)(2,1)} %refs_1_.1, bf16[320,640]{1,0:T(8,128)(2,1)} %refs_2_.1, bf16[320,640]{1,0:T(8,128)(2,1)} %bitcast.3, bf16[640]{0:T(1024)(128)(2,1)} %refs_4_.1), custom_call_target="tpu_custom_call" | custom-call | tf_op jit(solution)/shard_map/pallas_call | solution.py:581
  137.4 2.7 %shard_map.77 = (bf16[320,256]{1,0:T(8,128)(2,1)}, f32[320,640]{1,0:T(8,128)}, f32[320,640]{1,0:T(8,128)}) custom-call(bf16[320,256]{1,0:T(8,128)(2,1)} %get-tuple-element.9.dx_ref, bf16[3,320,640]{2,1,0:T(8,128)(2,1)} %get-tuple-element.10.in_ref, bf16[3,320,640]{2,1,0:T(8,128)(2,1)} %get-tuple-element.11.out_ref), custom_call_target="tpu_custom_call" | custom-call | tf_op jit(solution)/shard_map/pallas_call | solution.py:645

commit v5 on v4

v5 whole, which is shorter than its diff:
```python
import math

import jax
import jax.numpy as jnp
from jax import lax
from jax.experimental import pallas as pl
from jax.experimental.pallas import tpu as pltpu
from jax.sharding import PartitionSpec as P

MESH = pl.DeviceIdType.MESH
ROOT_HALF = 0.7071067811865476
INV_ROOT_TWO_PI = 0.3989422804014327
BF16 = jnp.bfloat16
F32 = jnp.float32

NZ = 8
NT = 8
ROWS = 256
SH = 320
HF = SH // 2
QD = SH // 4
QR = ROWS // 2
FC = 640
PARTS = (pl.ds(0, HF), pl.ds(HF, HF))

TN = (((0,), (0,)), ((), ()))
NN = (((1,), (0,)), ((), ()))
NT_DIMS = (((1,), (1,)), ((), ()))


def dot(lhs, rhs, dims):
    return lax.dot_general(lhs, rhs, dims, preferred_element_type=F32)


def kernel(
    scale, x_hbm, dy_hbm, win_hbm, wout_hbm, bias_ref,
    dx_out, parts_i, parts_o,
    dx_v, xv, dyv, tv, xt, dyt, wi, wo,
    pre, pre_in, act, gp, slope,
    term_g, term_i, rin_g, rin_i, lin_g, lin_i, dwo, dwo_in, dwo_v,
    dxa, dxb, sum_a, sum_b, in_a, in_b, last_a, last_b, turn_v, bias_in,
    ld_sem, sw_s, sw_r, ag_s, ag_r, ex_s, ex_r, core_s, core_r,
    rs_s, rs_r, own_s, own_r, dx_s, dx_r, dz_s, dz_r, dy_s, dy_r,
):
    dp = lax.axis_index("dp")
    tn = lax.axis_index("tensor")
    z, a = lax.div(dp, 2), lax.rem(dp, 2)
    t2, b = lax.div(tn, 2), lax.rem(tn, 2)
    x_, ypar = lax.div(t2, 2), lax.rem(t2, 2)
    y_ = 2 * a + ypar
    same = a == b
    differ = a != b
    zr, zl = lax.rem(z + 1, NZ), lax.rem(z + NZ - 1, NZ)

    def dev(z_, t_, a_, b_):
        return {"dp": 2 * z_ + a_, "tensor": 2 * t_ + b_}

    right, left = dev(zr, t2, a, b), dev(zl, t2, a, b)
    other_core = dev(z, t2, a, 1 - b)
    y_side = dev(z, t2 + 1 - 2 * ypar, 1 - a, b)

    def x_peer(r):
        return lax.rem(x_ + r, 4)

    def y_peer(r):
        yy = lax.rem(y_ + r, 4)
        return lax.rem(yy, 2), lax.div(yy, 2)

    def x_dev(r):
        return dev(z, 2 * x_peer(r) + ypar, a, b)

    def y_dev(r):
        yl, ah = y_peer(r)
        return dev(z, 2 * x_ + yl, ah, b)

    def rc(src, dst, ss, rs, to):
        return pltpu.make_async_remote_copy(
            src_ref=src, dst_ref=dst, send_sem=ss, recv_sem=rs, device_id=to, device_id_type=MESH
        )

    def part_rows(p):
        if isinstance(p, int):
            return PARTS[p]
        return pl.ds(pl.multiple_of(p * HF, HF), HF)

    hbm = (win_hbm, wout_hbm)
    weights = (wi, wo)
    here = part_rows(b)

    def ld_w(w):
        return pltpu.make_async_copy(hbm[w].at[here], weights[w].at[(0, b)[w], part_rows(a)], ld_sem.at[2 + w])

    ld_x = pltpu.make_async_copy(x_hbm, xv, ld_sem.at[0])
    ld_dy = pltpu.make_async_copy(dy_hbm, dyv, ld_sem.at[1])
    put_dx = pltpu.make_async_copy(dx_v, dx_out, ld_sem.at[4])

    @pl.when(same)
    def _():
        ld_w(0).start()
        ld_w(1).start()

    pl.when(same)(ld_dy.start)
    ld_x.start()

    barrier = pltpu.get_barrier_semaphore()

    def greet(to):
        pl.semaphore_signal(barrier, inc=1, device_id=to, device_id_type=MESH)

    for z_ in (zr, zl):
        greet(dev(z_, t2, a, b))
        greet(dev(z_, t2, a, 1 - b))
    for d in range(2, 7):
        greet(dev(lax.rem(z + d, NZ), t2, a, b))
    greet(other_core)
    greet(dev(z, t2, 1 - a, b))
    greet(dev(z, t2, 1 - a, 1 - b))
    for r in (1, 2, 3):
        greet(x_dev(r))
    greet(y_dev(1))
    greet(y_dev(3))
    pl.semaphore_wait(barrier, 17)

    def to_twin(w):
        rows = part_rows(a)
        return rc(hbm[w].at[part_rows(1 - b)], weights[w].at[(0, 1 - b)[w], rows], sw_s.at[2 * w], sw_r.at[2 * w], other_core)

    def to_chip(w, h):
        rows = part_rows(a)
        return rc(
            hbm[w].at[part_rows(h)], weights[w].at[(0, h)[w], rows], sw_s.at[2 * w + h], sw_r.at[2 * w + 1], dev(z, t2, b, h)
        )

    def from_twin(w):
        return rc(hbm[w].at[here], weights[w].at[(0, b)[w], part_rows(a)], sw_s.at[2 * w], sw_r.at[2 * w], other_core)

    def from_chip(w):
        return rc(hbm[w].at[here], weights[w].at[(0, b)[w], part_rows(1 - a)], sw_s.at[2 * w], sw_r.at[2 * w + 1], other_core)

    @pl.when(same)
    def _():
        to_twin(0).start()

    @pl.when(differ)
    def _():
        for h in range(2):
            to_chip(0, h).start()

    gathered = (wi, act)

    def piece(w, part):
        size = (HF, QR)[w]
        if isinstance(part, int):
            return pl.ds(part * size, size)
        return pl.ds(pl.multiple_of(part * size, size), size)

    def ag(w, g, s, part):
        buf, rows = gathered[w], piece(w, part)
        if g == 0:
            src, dst, to = s - 1, s, right
        else:
            src, dst, to = (NZ + 1 - s) % NZ, NZ - s, left
        i = ((w * 2 + g) * 4 + s - 1) * 2 + part
        return rc(buf.at[src, rows], buf.at[dst, rows], ag_s.at[i], ag_r.at[i], to)

    def send_first(part):
        for g in range(2):
            ag(0, g, 1, part).start()

    @pl.when(same)
    def _():
        ld_w(0).wait()

    @pl.when(differ)
    def _():
        from_twin(0).wait_recv()

    send_first(a)

    xh, xq = lax.div(x_, 2), lax.rem(x_, 2)
    cut_rows = pl.ds(pl.multiple_of(SH * xq + HF * xh + QD * ypar, QD), QD)
    FAR, NEAR = pl.ds(4, 4), pl.ds(0, 4)

    def dy_z(d):
        to = dev(lax.rem(z + d, NZ), t2, a, b)
        return rc(tv.at[d, cut_rows], dyt.at[(d + 2) % NZ, xh, xq, ypar], dz_s.at[d], dz_r.at[d], to)

    def dy_msg(kind, r, batch, tail, to):
        m = kind * 3 + r - 1
        ref = dyt.at[(batch,) + tail]
        return rc(ref, ref, dy_s.at[m], dy_r.at[m], to)

    def far_y(r):
        return dy_msg(0, r, FAR, (xh, xq, ypar), y_dev(r))

    def far_y_in(r):
        return dy_msg(0, r, FAR, (xh, xq, lax.rem(y_ + 4 - r, 2)), y_dev(r))

    def far_x(r):
        return dy_msg(1, r, FAR, (xh, xq), x_dev(r))

    def far_x_in(r):
        xs = lax.rem(x_ + 4 - r, 4)
        return dy_msg(1, r, FAR, (lax.div(xs, 2), lax.rem(xs, 2)), x_dev(r))

    def near_x(r):
        return dy_msg(2, r, NEAR, (xh, xq, ypar), x_dev(r))

    def near_x_in(r):
        xs = lax.rem(x_ + 4 - r, 4)
        return dy_msg(2, r, NEAR, (lax.div(xs, 2), lax.rem(xs, 2), ypar), x_dev(r))

    whole = pl.ds(0, 2)

    def near_y(r):
        return dy_msg(3, r, NEAR, (whole, whole, ypar), y_dev(r))

    def near_y_in(r):
        return dy_msg(3, r, NEAR, (whole, whole, lax.rem(y_ + 4 - r, 2)), y_dev(r))

    def from_source(r, wait):
        pl.when(lax.div(lax.rem(y_ + 4 - r, 4), 2) == b)(wait)

    @pl.when(same)
    def _():
        ld_dy.wait()

        def turn_dy(d, carry):
            k = lax.rem(z + d, NZ)
            tv[d] = dyv[:, pl.ds(pl.multiple_of(k * 2 * SH, 128), 2 * SH)].T
            return carry

        lax.fori_loop(0, NZ, turn_dy, 0)
        for d in (4, 3, 5, 2, 6, 1, 7):
            dy_z(d).start()
        dyt[2, xh, xq, ypar] = tv[0, cut_rows]

    bias_in[0] = jnp.broadcast_to(bias_ref[...].astype(F32)[None, :], (8, FC))
    bias_cp = rc(bias_in.at[0], bias_in.at[1], core_s.at[2], core_r.at[2], other_core)
    bias_cp.start()

    quads = ((0, 1, 7, 2), (6, 3, 5, 4))

    def at_x(i, x):
        p, q, r, t = quads[i]
        return jnp.where(x < 2, jnp.where(x == 0, p, q), jnp.where(x == 2, r, t))

    def turn(src, dst, d):
        k = lax.rem(z + NZ - d, NZ)
        v = src[:, pl.ds(pl.multiple_of(k * 2 * SH, 128), 2 * SH)].T
        first = b == 0
        dst[d, a, PARTS[0]] = jnp.where(first, v[:HF], v[HF:SH])
        dst[d, a, PARTS[1]] = jnp.where(first, v[SH : SH + HF], v[SH + HF :])

    def ex_y(i):
        ref = xt.at[at_x(i, x_), a]
        return rc(ref, ref, ex_s.at[i], ex_r.at[i], y_side)

    def ex_y_in(i):
        ref = xt.at[at_x(i, x_), 1 - a]
        return rc(ref, ref, ex_s.at[i], ex_r.at[i], y_side)

    def ex_x(i, r):
        ref, m = xt.at[at_x(i, x_), 1 - a], 1 + 3 * i + r
        return rc(ref, ref, ex_s.at[m], ex_r.at[m], x_dev(r))

    def ex_x_in(i, r):
        ref, m = xt.at[at_x(i, lax.rem(x_ + 4 - r, 4)), 1 - a], 1 + 3 * i + r
        return rc(ref, ref, ex_s.at[m], ex_r.at[m], x_dev(r))

    ld_x.wait()
    for d in range(NZ):
        turn(xv, xt, d)

    from_chip(0).wait_recv()
    send_first(1 - a)

    @pl.when(same)
    def _():
        for d in (4, 3, 5, 2):
            dy_z(d).wait_recv()
        for r in (1, 3, 2):
            far_y(r).start()
        for d in (6, 1, 7):
            dy_z(d).wait_recv()
        for r in (1, 3, 2):
            near_x(r).start()

    def pass_on(i):
        ex_y_in(i).wait_recv()
        for r in (1, 3, 2):
            ex_x(i, r).start()

    def step(w, s, part):
        for g in range(2):
            ag(w, g, s, part).wait_recv()
            ag(w, g, s + 1, part).start()

    def accumulate(acc, src, w, slots, first=False):
        n = len(slots)

        def body(i, carry):
            j, h = lax.div(i, 2), lax.rem(i, 2)
            d = slots[0] if n == 1 else slots[0] + j * (slots[1] - slots[0])
            acc[h] += dot(src[d, h], w[d], TN)
            return carry

        if first:
            acc[...] = jnp.zeros_like(acc)
        lax.fori_loop(0, 2 * n, body, 0)

    firsts = (0, 1)
    seconds = (1, 0)

    terms, rins, lins = (term_g, term_i), (rin_g, rin_i), (lin_g, lin_i)

    def make_terms(w, lo, hi):
        def body(i, carry):
            d = lax.rem(4 + lax.div(i + 1, 2) * (2 * lax.rem(i, 2) - 1) + NZ, NZ)
            if w == 0:
                j = lax.rem(d + 2, NZ)
                total = dot(dyt[j, 0].reshape(SH, ROWS), wo[0], TN) + dot(dyt[j, 1].reshape(SH, ROWS), wo[1], TN)
            else:
                total = (dot(xt[d, 0], gp[0], NN) + dot(xt[d, 1], gp[1], NN)) * scale
            terms[w][d] = total.astype(BF16)
            return carry

        lax.fori_loop(lo, hi, body, 0)

    def rs(w, g, e, part, last=False):
        rows = piece(1 - w, part)
        src = terms[w].at[NZ - e if g == 0 else e, rows]
        i = ((w * 2 + g) * 4 + e - 1) * 2 + part
        if last:
            m = 4 + (w * 2 + g) * 2 + b
            return rc(src, parts_i.at[1 + g, here], rs_s.at[i], own_r.at[m], dev((zr, zl)[g], t2, a, a))
        return rc(src, (rins, lins)[g][w].at[e - 1, rows], rs_s.at[i], rs_r.at[i], (right, left)[g])

    def last_in(w, g, h):
        m = 4 + (w * 2 + g) * 2 + h
        return rc(terms[w].at[0, PARTS[h]], parts_i.at[1 + g, PARTS[h]], own_s.at[0], own_r.at[m], right)

    def hop(w, g, e, part, last=False):
        rs(w, g, e + 1, part).wait_recv()
        d, rows = NZ - e if g == 0 else e, piece(1 - w, part)
        buf, came = terms[w], (rins, lins)[g][w]
        buf[d, rows] = (buf[d, rows].astype(F32) + came[e, rows].astype(F32)).astype(BF16)
        rs(w, g, e, part, last).start()

    def end_src(w, part):
        return dwo_v.at[part_rows(part)] if w == 0 else term_i.at[0, part_rows(part)]

    def end_dst(w, rows):
        return parts_o.at[rows] if w == 0 else parts_i.at[0, rows]

    def end_copy(w, part):
        m = 2 * w + part
        return rc(end_src(w, part), end_dst(w, here), own_s.at[m], own_r.at[2 * w + b], dev(z, t2, part, a))

    def end_local(w):
        return pltpu.make_async_copy(end_src(w, a), end_dst(w, here), own_s.at[2 * w + a])

    def end_in(w, h):
        return rc(end_src(w, h), end_dst(w, PARTS[h]), own_s.at[0], own_r.at[2 * w + h], right)

    def send_own(w):
        @pl.when(same)
        def _():
            end_local(w).start()

        @pl.when(differ)
        def _():
            end_copy(w, a).start()

    def send_sum():
        rows = part_rows(1 - a)
        for g in range(2):
            rs(1, g, 1, 1 - a).wait_recv()
        total = term_i[0, rows].astype(F32)
        for came in (rin_i, lin_i):
            total = total + came[0, rows].astype(F32)
        term_i[0, rows] = total.astype(BF16)
        end_copy(1, 1 - a).start()

    def wait_end(w):
        @pl.when(same)
        def _():
            end_local(w).wait()
            if w == 1:
                for g in range(2):
                    for h in range(2):
                        last_in(1, g, h).wait_recv()

        @pl.when(differ)
        def _():
            end_copy(w, a).wait_send()

        end_copy(w, 1 - a).wait_send()
        for h in range(2):
            @pl.when(jnp.logical_not(same & (b == h)))
            def _():
                end_in(w, h).wait_recv()

    step(0, 1, a)
    for r in (1, 2, 3):
        from_source(r, far_y_in(r).wait_recv)
    for r in (1, 3, 2):
        far_x(r).start()
    for i in range(2):
        ex_y(i).start()

    @pl.when(same)
    def _():
        to_twin(1).start()

    @pl.when(differ)
    def _():
        for h in range(2):
            to_chip(1, h).start()

    step(0, 1, 1 - a)
    for part in (a, 1 - a):
        for g in range(2):
            ag(0, g, 2, part).wait_recv()
    for pick in (firsts, seconds):
        for g in range(2):
            ag(0, g, 3, pick[g]).start()
    pass_on(0)

    @pl.when(same)
    def _():
        for r in (1, 2, 3):
            near_x_in(r).wait_recv()
        for r in (1, 3, 2):
            near_y(r).start()

    @pl.when(same)
    def _():
        ld_w(1).wait()

    @pl.when(differ)
    def _():
        from_twin(1).wait_recv()

    from_chip(1).wait_recv()
    wo_cp = rc(wo.at[b], wo.at[b], core_s.at[1], core_r.at[1], other_core)
    wo_in = rc(wo.at[1 - b], wo.at[1 - b], core_s.at[1], core_r.at[1], other_core)
    wo_cp.start()
    for g in range(2):
        ag(0, g, 3, firsts[g]).wait_recv()
        ag(0, g, 4, firsts[g]).start()
    pass_on(1)
    wo_in.wait_recv()
    for r in (1, 2, 3):
        far_x_in(r).wait_recv()
    make_terms(0, 0, 3)
    for g in range(2):
        rs(0, g, 4, firsts[g]).start()
    for g in range(2):
        rs(0, g, 3, seconds[g]).start()
    for r in (1, 2, 3):
        ex_x_in(0, r).wait_recv()
    accumulate(pre, xt, wi, (0,), True)
    accumulate(pre, xt, wi, (1, 7))
    accumulate(pre, xt, wi, (2,))
    for g in range(2):
        hop(0, g, 3, firsts[g])
    for g in range(2):
        ag(0, g, 3, seconds[g]).wait_recv()
    for r in (1, 2, 3):
        ex_x_in(1, r).wait_recv()
    accumulate(pre, xt, wi, (6,))
    accumulate(pre, xt, wi, (3, 5))
    for g in range(2):
        ag(0, g, 4, firsts[g]).wait_recv()
    accumulate(pre, xt, wi, (4,))
    pre_cp = rc(pre.at[1 - b], pre_in, core_s.at[0], core_r.at[0], other_core)
    pre_cp.start()
    for r in (1, 2, 3):
        from_source(r, near_y_in(r).wait_recv)
    make_terms(0, 3, 5)
    for g in range(2):
        hop(0, g, 2, seconds[g])
    bias_cp.wait_recv()
    bias = jnp.where(same, bias_in[0], bias_in[1])[0:1]
    pre_cp.wait_recv()

    def gelu(i, carry):
        rows = pl.ds(pl.multiple_of(i * 32, 32), 32)
        v = pre[b, rows] + pre_in[rows] + bias
        cdf = 0.5 * (1.0 + lax.erf(v * ROOT_HALF))
        act[0, rows] = (v * cdf).astype(BF16)
        slope[rows] = cdf + v * jnp.exp(-0.5 * v * v) * INV_ROOT_TWO_PI
        return carry

    lax.fori_loop(0, 8, gelu, 0)

    for pick in (firsts, seconds):
        for g in range(2):
            ag(1, g, 1, pick[g]).start()
    for g in range(2):
        hop(0, g, 2, firsts[g])
    make_terms(0, 5, 8)

    def add_out(slots, first=False):
        n = len(slots)

        def body(i, carry):
            q, h = lax.div(i, 2), lax.rem(i, 2)
            d = slots[0] if n == 1 else slots[0] + q * (slots[1] - slots[0])
            j = (slots[0] + 2) % NZ if n == 1 else lax.rem(d + 2, NZ)
            dwo[h] += dot(dyt[j, h].reshape(SH, ROWS), act[d], NN)
            return carry

        if first:
            dwo[...] = jnp.zeros_like(dwo)
        lax.fori_loop(0, 2 * n, body, 0)

    def pass_act(s, picks):
        for pick in picks:
            for g in range(2):
                ag(1, g, s, pick[g]).wait_recv()
                ag(1, g, s + 1, pick[g]).start()

    pass_act(1, (firsts, seconds))
    for pick in (seconds, firsts):
        for g in range(2):
            hop(0, g, 1, pick[g])
    add_out((0,), True)
    add_out((1, 7))
    pass_act(2, (firsts, seconds))
    add_out((2, 6))
    for pick in (seconds, firsts):
        for g in range(2):
            rs(0, g, 1, pick[g]).wait_recv()

    def grad(i, carry):
        rows = pl.ds(pl.multiple_of(i * 32, 32), 32)
        v = term_g[0, rows].astype(F32) + rin_g[0, rows].astype(F32) + lin_g[0, rows].astype(F32)
        gp[b, rows] = (v * slope[rows]).astype(BF16)
        return carry

    lax.fori_loop(0, 8, grad, 0)
    gp_cp = rc(gp.at[b], gp.at[b], core_s.at[4], core_r.at[4], other_core)
    gp_cp.start()
    rc(gp.at[1 - b], gp.at[1 - b], core_s.at[4], core_r.at[4], other_core).wait_recv()
    make_terms(1, 0, 3)
    for g in range(2):
        rs(1, g, 4, firsts[g]).start()
    for g in range(2):
        rs(1, g, 3, seconds[g]).start()

    def dx_body(i, carry):
        k, h = lax.div(i, 2), lax.rem(i, 2)
        d = lax.rem(z + NZ - k, NZ)
        v = dot(wi[d], gp[h], NT_DIMS).astype(BF16)
        xx, yy = lax.div(k, 2), 2 * lax.rem(k, 2) + h
        dxa[xx, yy] = v[:HF]
        dxb[yy, xx] = v[HF:]
        return carry

    lax.fori_loop(0, 16, dx_body, 0)
    yy_ = 2 * ypar + a

    def y_index(r):
        yl, ah = y_peer(r)
        return 2 * yl + ah

    def first_a(r):
        return rc(dxa.at[x_peer(r)], in_a.at[r - 1], dx_s.at[r - 1], dx_r.at[r - 1], x_dev(r))

    def first_b(r):
        return rc(dxb.at[y_index(r)], in_b.at[r - 1], dx_s.at[r + 2], dx_r.at[r + 2], y_dev(r))

    def second_a(r):
        return rc(sum_a.at[y_index(r)], last_a.at[r - 1], dx_s.at[r + 5], dx_r.at[r + 5], y_dev(r))

    def second_b(r):
        return rc(sum_b.at[x_peer(r)], last_b.at[r - 1], dx_s.at[r + 8], dx_r.at[r + 8], x_dev(r))

    for r in (1, 2, 3):
        first_a(r).start()
        first_b(r).start()

    for g in range(2):
        hop(1, g, 3, firsts[g])
    pass_act(3, (firsts,))
    make_terms(1, 3, 8)
    send_own(1)
    for part in (1 - a, a):
        for g in range(2):
            hop(1, g, 2, part)

    for g in range(2):
        ag(1, g, 3, seconds[g]).wait_recv()
    add_out((3, 5))
    for g in range(2):
        ag(1, g, 4, firsts[g]).wait_recv()
    add_out((4,))
    dwo_cp = rc(dwo.at[1 - b], dwo_in, core_s.at[5], core_r.at[5], other_core)
    dwo_cp.start()
    for g in range(2):
        hop(1, g, 1, 1 - a)
    dwo_cp.wait_recv()
    dwo_v[...] = ((dwo[b] + dwo_in[...]) * scale).astype(BF16)
    send_own(0)
    end_copy(0, 1 - a).start()

    for r in (1, 2, 3):
        first_a(r).wait_recv()
        first_b(r).wait_recv()

    def sum_body(i, carry):
        total_a, total_b = dxa[x_, i].astype(F32), dxb[yy_, i].astype(F32)
        for r in range(3):
            total_a = total_a + in_a[r, i].astype(F32)
            total_b = total_b + in_b[r, i].astype(F32)
        sum_a[i], sum_b[i] = total_a.astype(BF16), total_b.astype(BF16)
        return carry

    lax.fori_loop(0, 4, sum_body, 0)
    for r in (1, 2, 3):
        second_a(r).start()
        second_b(r).start()

    for g in range(2):
        hop(1, g, 1, a, True)
    send_sum()

    for r in (1, 2, 3):
        second_a(r).wait_recv()
        second_b(r).wait_recv()
    total_a, total_b = sum_a[yy_].astype(F32), sum_b[x_].astype(F32)
    for r in range(3):
        total_a = total_a + last_a[r].astype(F32)
        total_b = total_b + last_b[r].astype(F32)
    total_a, total_b = total_a.astype(BF16), total_b.astype(BF16)
    dx_v[here] = jnp.where(b == 0, total_a, total_b)
    turn_v[...] = jnp.where(b == 0, total_b, total_a)
    dx_cp = rc(turn_v, dx_v.at[here], core_s.at[3], core_r.at[3], other_core)
    dx_cp.start()

    rc(turn_v, dx_v.at[part_rows(1 - b)], core_s.at[3], core_r.at[3], other_core).wait_recv()
    put_dx.start()


    @pl.when(same)
    def _():
        to_twin(0).wait_send()
        to_twin(1).wait_send()

    @pl.when(differ)
    def _():
        for w in range(2):
            for h in range(2):
                to_chip(w, h).wait_send()

    for w in range(2):
        for g in range(2):
            for s in (1, 2, 3):
                for part in range(2):
                    ag(w, g, s, part).wait_send()
            ag(w, g, 4, firsts[g]).wait_send()
    for i in range(2):
        ex_y(i).wait_send()
        for r in (1, 2, 3):
            ex_x(i, r).wait_send()
    for r in (1, 2, 3):
        far_x(r).wait_send()

    @pl.when(same)
    def _():
        for d in range(1, NZ):
            dy_z(d).wait_send()
        for r in (1, 2, 3):
            far_y(r).wait_send()
            near_x(r).wait_send()
            near_y(r).wait_send()

    for cp in (bias_cp, pre_cp, wo_cp, gp_cp, dwo_cp):
        cp.wait_send()
    for w in range(2):
        for g in range(2):
            rs(w, g, 4, firsts[g]).wait_send()
            for e in (3, 2) if w else (3, 2, 1):
                for part in range(2):
                    rs(w, g, e, part).wait_send()
    for r in (1, 2, 3):
        for cp in (first_a(r), first_b(r), second_a(r), second_b(r)):
            cp.wait_send()

    wait_end(0)
    wait_end(1)
    for g in range(2):
        for part in range(2):
            rs(1, g, 1, part).wait_send()
    dx_cp.wait_send()
    put_dx.wait()


def finish(dx_ref, in_ref, out_ref, dx_out, dwin_out, dwout_out):
    dx_out[...] = dx_ref[...]
    whole = lax.rem(lax.axis_index("dp"), 2) != lax.rem(lax.axis_index("tensor"), 2)
    dwout_out[...] = out_ref[...].astype(F32)

    @pl.when(whole)
    def _():
        dwin_out[...] = in_ref[0].astype(F32)

    @pl.when(jnp.logical_not(whole))
    def _():
        dwin_out[...] = in_ref[0].astype(F32) + in_ref[1].astype(F32) + in_ref[2].astype(F32)


def per_device(inputs, upstream, w_in, bias_in, w_out):
    rows, width = inputs.shape
    scale = 1.0 / math.sqrt(rows * lax.axis_size("dp"))
    any_space = pl.BlockSpec(memory_space=pl.ANY)
    vmem = pl.BlockSpec(memory_space=pltpu.VMEM)
    shard = (SH, FC)
    ring = (NZ,) + shard
    acc = (2, ROWS, FC)
    half = (ROWS, FC)
    turned = (NZ, 2, SH, ROWS)
    dx, parts_i, parts_o = pl.pallas_call(
        lambda *refs: kernel(scale, *refs),
        out_shape=(
            jax.ShapeDtypeStruct((SH, ROWS), BF16),
            jax.ShapeDtypeStruct((3,) + shard, BF16),
            jax.ShapeDtypeStruct(shard, BF16),
        ),
        in_specs=[any_space, any_space, any_space, any_space, vmem],
        out_specs=(any_space, any_space, any_space),
        scratch_shapes=[
            pltpu.VMEM((SH, ROWS), BF16),
            pltpu.VMEM((rows, width), BF16),
            pltpu.VMEM((rows, width), BF16),
            pltpu.VMEM((NZ, 2 * SH, ROWS), BF16),
            pltpu.VMEM(turned, BF16),
            pltpu.VMEM((NZ, 2, 2, 2, QD, ROWS), BF16),
            pltpu.VMEM(ring, BF16),
            pltpu.VMEM((2,) + shard, BF16),
            pltpu.VMEM(acc, F32),
            pltpu.VMEM(half, F32),
            pltpu.VMEM((NZ,) + half, BF16),
            pltpu.VMEM(acc, BF16),
            pltpu.VMEM(half, F32),
            pltpu.VMEM((NZ,) + half, BF16),
            pltpu.VMEM(ring, BF16),
            pltpu.VMEM((4,) + half, BF16),
            pltpu.VMEM((4,) + shard, BF16),
            pltpu.VMEM((4,) + half, BF16),
            pltpu.VMEM((4,) + shard, BF16),
            pltpu.VMEM((2,) + shard, F32),
            pltpu.VMEM(shard, F32),
            pltpu.VMEM(shard, BF16),
            pltpu.VMEM((4, 4, HF, ROWS), BF16),
            pltpu.VMEM((4, 4, HF, ROWS), BF16),
            pltpu.VMEM((4, HF, ROWS), BF16),
            pltpu.VMEM((4, HF, ROWS), BF16),
            pltpu.VMEM((3, 4, HF, ROWS), BF16),
            pltpu.VMEM((3, 4, HF, ROWS), BF16),
            pltpu.VMEM((3, HF, ROWS), BF16),
            pltpu.VMEM((3, HF, ROWS), BF16),
            pltpu.VMEM((HF, ROWS), BF16),
            pltpu.VMEM((2, 8, FC), F32),
            pltpu.SemaphoreType.DMA((5,)),
            pltpu.SemaphoreType.DMA((4,)),
            pltpu.SemaphoreType.DMA((4,)),
            pltpu.SemaphoreType.DMA((32,)),
            pltpu.SemaphoreType.DMA((32,)),
            pltpu.SemaphoreType.DMA((16,)),
            pltpu.SemaphoreType.DMA((16,)),
            pltpu.SemaphoreType.DMA((6,)),
            pltpu.SemaphoreType.DMA((6,)),
            pltpu.SemaphoreType.DMA((32,)),
            pltpu.SemaphoreType.DMA((32,)),
            pltpu.SemaphoreType.DMA((4,)),
            pltpu.SemaphoreType.DMA((12,)),
            pltpu.SemaphoreType.DMA((12,)),
            pltpu.SemaphoreType.DMA((12,)),
            pltpu.SemaphoreType.DMA((8,)),
            pltpu.SemaphoreType.DMA((8,)),
            pltpu.SemaphoreType.DMA((12,)),
            pltpu.SemaphoreType.DMA((12,)),
        ],
        compiler_params=pltpu.CompilerParams(
            collective_id=0, has_side_effects=True, vmem_limit_bytes=60 * 1024 * 1024
        ),
    )(inputs, upstream, w_in, w_out.T, bias_in)
    steps = 2
    part_spec = pl.BlockSpec((3, SH // steps, FC), lambda i: (0, i, 0))
    dx_spec = pl.BlockSpec((SH // steps, ROWS), lambda i: (i, 0))
    dw_spec = pl.BlockSpec((SH // steps, FC), lambda i: (i, 0))
    dx, dwin, dwout = pl.pallas_call(
        finish,
        grid=(steps,),
        out_shape=(
            jax.ShapeDtypeStruct((SH, ROWS), BF16),
            jax.ShapeDtypeStruct(shard, F32),
            jax.ShapeDtypeStruct(shard, F32),
        ),
        in_specs=[dx_spec, part_spec, dw_spec],
        out_specs=(dx_spec, dw_spec, dw_spec),
    )(dx, parts_i, parts_o)
    return dx.T, dwin, dwout.T


def solution(mesh):
    placed = (P("dp", None), P("dp", None), P("dp", "tensor"), P("tensor"), P("tensor", "dp"))
    return jax.shard_map(
        per_device,
        mesh=mesh,
        in_specs=placed,
        out_specs=(P("dp", "tensor"), P("dp", "tensor"), P("tensor", "dp")),
        check_vma=False,
    )
```

time: 140 us -> 139 us (level)
    pallas_call x1, Pallas kernels: 137 us -> 135 us  [per_device(): pl.pallas_call(lambda *refs: kernel(scale, *refs), out_shape=(jax.ShapeDt...]
where the time goes in v5:
time: 139 us; the launch traced here: 138 us
  Pallas kernels  138 us (99%)
    pallas_call x1, Pallas kernels, per_device(): pl.pallas_call(lambda *refs: kernel(scale, *refs), out_shape=(jax.ShapeDt...  135 us

profile of v5, /device:TPU:1, one launch (start us, length us, event | category | flops | bytes accessed | tf_op | source)
XLA Modules:
  0.0 138.3 jit_solution(11736076882461999357)
XLA Ops:
  0.6 135.2 %shard_map.76 = (bf16[320,256]{1,0:T(8,128)(2,1)}, bf16[3,320,640]{2,1,0:T(8,128)(2,1)}, bf16[320,640]{1,0:T(8,128)(2,1)}) custom-call(bf16[256,5120]{1,0:T(8,128)(2,1)} %refs_0_.1, bf16[256,5120]{1,0:T(8,128)(2,1)} %refs_1_.1, bf16[320,640]{1,0:T(8,128)(2,1)} %refs_2_.1, bf16[320,640]{1,0:T(8,128)(2,1)} %bitcast.3, bf16[640]{0:T(1024)(128)(2,1)} %refs_4_.1), custom_call_target="tpu_custom_call" | custom-call | tf_op jit(solution)/shard_map/pallas_call | solution.py:725
  135.9 2.5 %shard_map.77 = (bf16[320,256]{1,0:T(8,128)(2,1)}, f32[320,640]{1,0:T(8,128)}, f32[320,640]{1,0:T(8,128)}) custom-call(bf16[320,256]{1,0:T(8,128)(2,1)} %get-tuple-element.9.dx_ref, bf16[3,320,640]{2,1,0:T(8,128)(2,1)} %get-tuple-element.10.in_ref, bf16[320,640]{1,0:T(8,128)(2,1)} %get-tuple-element.11.out_ref), custom_call_target="tpu_custom_call" | custom-call | tf_op jit(solution)/shard_map/pallas_call | solution.py:795

commit v6 on v5

--- a/solution.py
+++ b/solution.py
@@ -402,6 +402,7 @@
                 end_in(w, h).wait_recv()
 
     step(0, 1, a)
+    step(0, 1, 1 - a)
     for r in (1, 2, 3):
         from_source(r, far_y_in(r).wait_recv)
     for r in (1, 3, 2):
@@ -418,13 +419,8 @@
         for h in range(2):
             to_chip(1, h).start()
 
-    step(0, 1, 1 - a)
-    for part in (a, 1 - a):
-        for g in range(2):
-            ag(0, g, 2, part).wait_recv()
-    for pick in (firsts, seconds):
-        for g in range(2):
-            ag(0, g, 3, pick[g]).start()
+    step(0, 2, a)
+    step(0, 2, 1 - a)
     pass_on(0)
 
     @pl.when(same)
@@ -458,13 +454,18 @@
         rs(0, g, 4, firsts[g]).start()
     for g in range(2):
         rs(0, g, 3, seconds[g]).start()
+    for g in range(2):
+        hop(0, g, 3, firsts[g])
     for r in (1, 2, 3):
         ex_x_in(0, r).wait_recv()
     accumulate(pre, xt, wi, (0,), True)
     accumulate(pre, xt, wi, (1, 7))
     accumulate(pre, xt, wi, (2,))
-    for g in range(2):
-        hop(0, g, 3, firsts[g])
+    for r in (1, 2, 3):
+        from_source(r, near_y_in(r).wait_recv)
+    make_terms(0, 3, 5)
+    for g in range(2):
+        hop(0, g, 2, seconds[g])
     for g in range(2):
         ag(0, g, 3, seconds[g]).wait_recv()
     for r in (1, 2, 3):
@@ -476,11 +477,8 @@
     accumulate(pre, xt, wi, (4,))
     pre_cp = rc(pre.at[1 - b], pre_in, core_s.at[0], core_r.at[0], other_core)
     pre_cp.start()
-    for r in (1, 2, 3):
-        from_source(r, near_y_in(r).wait_recv)
-    make_terms(0, 3, 5)
-    for g in range(2):
-        hop(0, g, 2, seconds[g])
+    for g in range(2):
+        hop(0, g, 2, firsts[g])
     bias_cp.wait_recv()
     bias = jnp.where(same, bias_in[0], bias_in[1])[0:1]
     pre_cp.wait_recv()
@@ -498,8 +496,6 @@
     for pick in (firsts, seconds):
         for g in range(2):
             ag(1, g, 1, pick[g]).start()
-    for g in range(2):
-        hop(0, g, 2, firsts[g])
     make_terms(0, 5, 8)
 
     def add_out(slots, first=False):

time: 139 us -> 137 us (0.986)
  Pallas kernels: 138 us -> 136 us
    pallas_call x1, Pallas kernels: 135 us -> 134 us  [per_device(): pl.pallas_call(lambda *refs: kernel(scale, *refs), out_shape=(jax.ShapeDt...]
where the time goes in v6:
time: 137 us
  Pallas kernels  136 us (99%)
    pallas_call x1, Pallas kernels, per_device(): pl.pallas_call(lambda *refs: kernel(scale, *refs), out_shape=(jax.ShapeDt...  134 us

profile of v6, /device:TPU:1, one launch (start us, length us, event | category | flops | bytes accessed | tf_op | source)
XLA Modules:
  0.0 136.8 jit_solution(8863305716250406587)
XLA Ops:
  0.6 133.7 %shard_map.76 = (bf16[320,256]{1,0:T(8,128)(2,1)}, bf16[3,320,640]{2,1,0:T(8,128)(2,1)}, bf16[320,640]{1,0:T(8,128)(2,1)}) custom-call(bf16[256,5120]{1,0:T(8,128)(2,1)} %refs_0_.1, bf16[256,5120]{1,0:T(8,128)(2,1)} %refs_1_.1, bf16[320,640]{1,0:T(8,128)(2,1)} %refs_2_.1, bf16[320,640]{1,0:T(8,128)(2,1)} %bitcast.3, bf16[640]{0:T(1024)(128)(2,1)} %refs_4_.1), custom_call_target="tpu_custom_call" | custom-call | tf_op jit(solution)/shard_map/pallas_call | solution.py:721
  134.3 2.5 %shard_map.77 = (bf16[320,256]{1,0:T(8,128)(2,1)}, f32[320,640]{1,0:T(8,128)}, f32[320,640]{1,0:T(8,128)}) custom-call(bf16[320,256]{1,0:T(8,128)(2,1)} %get-tuple-element.9.dx_ref, bf16[3,320,640]{2,1,0:T(8,128)(2,1)} %get-tuple-element.10.in_ref, bf16[320,640]{1,0:T(8,128)(2,1)} %get-tuple-element.11.out_ref), custom_call_target="tpu_custom_call" | custom-call | tf_op jit(solution)/shard_map/pallas_call | solution.py:791

commit v7 on v6

--- a/solution.py
+++ b/solution.py
@@ -1,3 +1,4 @@
+import functools
 import math
 
 import jax
@@ -442,9 +443,15 @@
     wo_cp = rc(wo.at[b], wo.at[b], core_s.at[1], core_r.at[1], other_core)
     wo_in = rc(wo.at[1 - b], wo.at[1 - b], core_s.at[1], core_r.at[1], other_core)
     wo_cp.start()
-    for g in range(2):
+
+    def fourth(g):
         ag(0, g, 3, firsts[g]).wait_recv()
         ag(0, g, 4, firsts[g]).start()
+
+    for g in range(2):
+        pl.when(a == g)(functools.partial(fourth, g))
+    for g in range(2):
+        pl.when(a != g)(functools.partial(fourth, g))
     pass_on(1)
     wo_in.wait_recv()
     for r in (1, 2, 3):

time: 137 us -> 136 us (level)
  no operation moved by 1% of the time
where the time goes in v7:
time: 136 us
  Pallas kernels  136 us (100%)
    pallas_call x1, Pallas kernels, per_device(): pl.pallas_call(lambda *refs: kernel(scale, *refs), out_shape=(jax.ShapeDt...  133 us

profile of v7, /device:TPU:1, one launch (start us, length us, event | category | flops | bytes accessed | tf_op | source)
XLA Modules:
  0.0 136.3 jit_solution(9198298798173194809)
XLA Ops:
  0.6 133.2 %shard_map.76 = (bf16[320,256]{1,0:T(8,128)(2,1)}, bf16[3,320,640]{2,1,0:T(8,128)(2,1)}, bf16[320,640]{1,0:T(8,128)(2,1)}) custom-call(bf16[256,5120]{1,0:T(8,128)(2,1)} %refs_0_.1, bf16[256,5120]{1,0:T(8,128)(2,1)} %refs_1_.1, bf16[320,640]{1,0:T(8,128)(2,1)} %refs_2_.1, bf16[320,640]{1,0:T(8,128)(2,1)} %bitcast.3, bf16[640]{0:T(1024)(128)(2,1)} %refs_4_.1), custom_call_target="tpu_custom_call" | custom-call | tf_op jit(solution)/shard_map/pallas_call | solution.py:728
  133.9 2.5 %shard_map.77 = (bf16[320,256]{1,0:T(8,128)(2,1)}, f32[320,640]{1,0:T(8,128)}, f32[320,640]{1,0:T(8,128)}) custom-call(bf16[320,256]{1,0:T(8,128)(2,1)} %get-tuple-element.9.dx_ref, bf16[3,320,640]{2,1,0:T(8,128)(2,1)} %get-tuple-element.10.in_ref, bf16[320,640]{1,0:T(8,128)(2,1)} %get-tuple-element.11.out_ref), custom_call_target="tpu_custom_call" | custom-call | tf_op jit(solution)/shard_map/pallas_call | solution.py:798
